TPU v7x, 128 devices: a whole 4x4x4 slice. The times are simulated.
128 devices in a mesh: tok: 4 (over y_hi, core), wt: 32 (over x, z, y_lo).
Axes of the slice: x: 4, y: 4 (y_hi: 2, y_lo: 2; y = y_hi * 2 + y_lo), z: 4, core: 2. Of those that a mesh axis runs over, the one named last changes fastest.
Arguments:
- activations: bfloat16 [1536, 8192], P('tok', 'wt'), may hold values from -6 to 6
- gate_pre: bfloat16 [1536, 16384], P('tok', 'wt'), may hold values from -6 to 6
- up_pre: bfloat16 [1536, 16384], P('tok', 'wt'), may hold values from -6 to 6
- hidden_grad: bfloat16 [1536, 16384], P('tok', 'wt'), may hold values from -0.59765625 to 0.59765625
- gate_blocks: bfloat16 [4096, 128, 128], P('wt'), may hold values from -0.125 to 0.125
- up_blocks: bfloat16 [4096, 128, 128], P('wt'), may hold values from -0.125 to 0.125
- block_rows: int32 [4096], P('wt'), may hold values from 0 to 127, as said below
- block_cols: int32 [4096], P('wt'), may hold values from 0 to 63, as said below
- block_count: int32 [32], P('wt'), may hold values from 32 to 128, as said below
Outputs:
- input_grad: bfloat16 [1536, 8192], P('tok', 'wt')
- gate_weight_grad: bfloat16 [4096, 128, 128], P('wt')
- up_weight_grad: bfloat16 [4096, 128, 128], P('wt')
Inputs may be any that keep to these rules, and one draw needn't show every extreme that they name: `block_rows`: slots of wt index w are w * 128 to (w + 1) * 128 - 1; their block rows lie in w * 4 to (w + 1) * 4 - 1; slots past the count repeat the owner's first slot. `block_cols`: the live slots of one owner name distinct blocks. `block_count`: one owner holds exactly 128 kept blocks.
All inputs are finite; a program needn't handle non-finite values.
Results may differ from a plain program's by a relative error of at most 0.025.
Values may be sent and summed in bfloat16 or wider, within the bound.
No kernel may reach another device: no remote copies, remote signals or barrier semaphores. Data moves between devices by JAX's collectives and lax.ppermute only.
A program may use at most 192 MiB of HBM per device.

v0:
```python
import jax
import jax.numpy as jnp
from jax import lax
from jax.sharding import PartitionSpec as P


def body(
    activations,
    gate_pre,
    up_pre,
    hidden_grad,
    gate_blocks,
    up_blocks,
    block_rows,
    block_cols,
    block_count,
):
    gate_value = gate_pre.astype(jnp.float32)
    up_value = up_pre.astype(jnp.float32)
    grad_value = hidden_grad.astype(jnp.float32)
    sigmoid_gate = jax.nn.sigmoid(gate_value)
    gate_grad = (
        grad_value * up_value * sigmoid_gate * (1.0 + gate_value * (1.0 - sigmoid_gate))
    ).astype(jnp.bfloat16)
    up_grad = (grad_value * gate_value * sigmoid_gate).astype(jnp.bfloat16)
    tok_rows = gate_grad.shape[0]
    slot_total = gate_blocks.shape[0]
    width = gate_blocks.shape[1]
    owned = gate_grad.shape[1] // width
    gathered = lax.all_gather(activations, "wt", axis=1, tiled=True)
    col_total = gathered.shape[1] // width
    local_rows = block_rows % owned
    alive = jnp.arange(slot_total, dtype=jnp.int32) < block_count[0]
    mask = alive[:, None, None]
    gate_kept = jnp.where(mask, gate_blocks, jnp.zeros_like(gate_blocks))
    up_kept = jnp.where(mask, up_blocks, jnp.zeros_like(up_blocks))
    target = local_rows * col_total + block_cols

    def densify(kept):
        grid = jnp.zeros((owned * col_total, width, width), jnp.bfloat16).at[target].add(kept)
        grid = grid.reshape(owned, col_total, width, width).transpose(0, 2, 1, 3)
        return grid.reshape(owned * width, col_total * width)

    terms = jnp.dot(gate_grad, densify(gate_kept), preferred_element_type=jnp.float32)
    terms = terms + jnp.dot(up_grad, densify(up_kept), preferred_element_type=jnp.float32)
    input_grad = lax.psum_scatter(terms.astype(jnp.bfloat16), "wt", scatter_dimension=1, tiled=True)
    feature_sel = jnp.take(gathered.reshape(tok_rows, col_total, width), block_cols, axis=1)
    gate_sel = jnp.take(gate_grad.reshape(tok_rows, owned, width), local_rows, axis=1)
    up_sel = jnp.take(up_grad.reshape(tok_rows, owned, width), local_rows, axis=1)
    gate_part = jnp.einsum(
        "tsj,tsk->sjk", gate_sel, feature_sel, preferred_element_type=jnp.float32
    )
    up_part = jnp.einsum("tsj,tsk->sjk", up_sel, feature_sel, preferred_element_type=jnp.float32)
    gate_part = jnp.where(mask, gate_part, jnp.float32(0.0))
    up_part = jnp.where(mask, up_part, jnp.float32(0.0))
    gate_total, up_total = (
        lax.psum(gate_part.astype(jnp.bfloat16), "tok").astype(jnp.float32),
        lax.psum(up_part.astype(jnp.bfloat16), "tok").astype(jnp.float32),
    )
    gate_weight_grad = gate_total.astype(jnp.bfloat16)
    up_weight_grad = up_total.astype(jnp.bfloat16)
    return (input_grad, gate_weight_grad, up_weight_grad)


def solution(mesh):
    in_specs = (
        P("tok", "wt"),
        P("tok", "wt"),
        P("tok", "wt"),
        P("tok", "wt"),
        P("wt", None, None),
        P("wt", None, None),
        P("wt"),
        P("wt"),
        P("wt"),
    )
    out_specs = (P("tok", "wt"), P("wt", None, None), P("wt", None, None))
    return jax.shard_map(body, mesh=mesh, in_specs=in_specs, out_specs=out_specs, check_vma=False)
```

profile of v0, /device:TPU:0, one launch (start us, length us, event | category | flops | bytes accessed | tf_op | source)
XLA Modules:
  0.0 528.8 jit_solution(13295388391561334772)
XLA Ops:
  7.2 1.8 copy.20
  9.0 1.2 copy.16
  10.3 1.2 copy.14
  11.5 1.2 copy.15
  15.3 6.0 %broadcast_select_fusion.3 = (bf16[128,128,128]{2,1,0:T(8,128)(2,1)}, bf16[128,128,128]{2,1,0:T(8,128)(2,1)}) fusion(bf16[128,128,128]{2,1,0:T(8,128)(2,1)} %param.16, pred[128]{0:T(512)(128)(4,1)S(1)} %get-tuple-element.18, bf16[128,128,128]{2,1,0:T(8,128)(2,1)} %param.15), kind=kLoop, calls=%fused_computation.26 | loop fusion | flops 4194304 | bytes 16777344 | tf_op jit(solution)/shard_map/jit(_where)/select_n | solution.py:36
  21.4 5.3 %broadcast.30.clone = bf16[256,128,128]{2,1,0:T(8,128)(2,1)} broadcast(bf16[]{:T(256)} %constant.28.clone.1), dimensions={} | broadcast | bytes 8388610 | tf_op jit(solution)/shard_map/broadcast.9
  26.7 28.8 %scatter_fusion = bf16[256,128,128]{2,1,0:T(8,128)(2,1)} fusion(bf16[256,128,128]{2,1,0:T(8,128)(2,1)} %broadcast.30.clone, s32[128]{0:T(128)S(1)} %get-tuple-element.11, bf16[128,128,128]{2,1,0:T(8,128)(2,1)} %get-tuple-element.14), kind=kCustom, calls=%fused_computation.3 | custom fusion | flops 2097152 | bytes 12583424 | tf_op jit(solution)/shard_map/scatter-add | solution.py:40
  55.5 12.0 %copy.17 = bf16[4,128,64,128]{3,2,1,0:T(8,128)(2,1)} copy(bf16[4,128,64,128]{3,1,2,0:T(8,128)(2,1)} %bitcast.43) | data formatting | bytes 16777216 | tf_op jit(solution)/shard_map/transpose | solution.py:41
  67.5 5.3 %broadcast.30.clone.1 = bf16[256,128,128]{2,1,0:T(8,128)(2,1)} broadcast(bf16[]{:T(256)} %constant.28.clone.1), dimensions={} | broadcast | bytes 8388610 | tf_op jit(solution)/shard_map/broadcast.9
  72.8 28.9 %scatter_fusion.1 = bf16[256,128,128]{2,1,0:T(8,128)(2,1)} fusion(bf16[256,128,128]{2,1,0:T(8,128)(2,1)} %broadcast.30.clone.1, s32[128]{0:T(128)S(1)} %get-tuple-element.11, bf16[128,128,128]{2,1,0:T(8,128)(2,1)} %get-tuple-element.13), kind=kCustom, calls=%fused_computation.4 | custom fusion | flops 2097152 | bytes 12583424 | tf_op jit(solution)/shard_map/scatter-add | solution.py:40
  101.7 12.1 %copy.18 = bf16[4,128,64,128]{3,2,1,0:T(8,128)(2,1)} copy(bf16[4,128,64,128]{3,1,2,0:T(8,128)(2,1)} %bitcast.42) | data formatting | bytes 16777216 | tf_op jit(solution)/shard_map/transpose | solution.py:41
  114.2 14.5 %fusion.12 = f32[384,8192]{1,0:T(8,128)} fusion(bf16[384,512]{0,1:T(8,128)(2,1)S(1)} %get-tuple-element.9, bf16[64,8,64,128]{3,2,1,0:T(8,128)(2,1)} %bitcast.44), kind=kOutput, calls=%fused_computation.19 | convolution fusion | flops 3221225472 | bytes 21364736 | tf_op jit(solution)/shard_map/dot_general | solution.py:44
  128.8 16.4 %add_convert_fusion = bf16[384,8192]{1,0:T(8,128)(2,1)} fusion(f32[384,8192]{1,0:T(8,128)} %fusion.12, bf16[384,512]{0,1:T(8,128)(2,1)S(1)} %get-tuple-element.8, bf16[64,8,64,128]{3,2,1,0:T(8,128)(2,1)} %bitcast.45), kind=kOutput, calls=%fused_computation.13 | convolution fusion | flops 3227516928 | bytes 27656192 | tf_op jit(solution)/shard_map/dot_general | solution.py:45
  145.8 8.5 %gather_fusion.1 = bf16[128,384,128]{2,1,0:T(8,128)(2,1)} fusion(bf16[384,4,128]{2,0,1:T(8,128)(2,1)S(1)} %copy.19, s32[1024]{0:T(1024)S(1)} %get-tuple-element.16), kind=kCustom, calls=%fused_computation.clone | custom fusion | bytes 25166336 | tf_op jit(solution)/shard_map/jit(_take)/gather | solution.py:48
  154.2 8.2 %gather_fusion.2 = bf16[128,384,128]{2,1,0:T(8,128)(2,1)} fusion(bf16[384,4,128]{2,0,1:T(8,128)(2,1)S(1)} %copy.23, s32[1024]{0:T(1024)S(1)} %get-tuple-element.16), kind=kCustom, calls=%fused_computation.1.clone | custom fusion | bytes 25166336 | tf_op jit(solution)/shard_map/jit(_take)/gather | solution.py:49
  162.5 14.9 %all-gather.2.cloned.1.call-done = bf16[384,8192]{0,1:T(8,128)(2,1)} async-done(((bf16[384,256]{0,1:T(8,128)(2,1)}), bf16[384,8192]{0,1:T(8,128)(2,1)}) %all-gather.2.cloned.1.call-update) | async-done | bytes 6291472 | tf_op jit(solution)/shard_map/all_gather | solution.py:30
  177.4 8.7 %copy.21 = bf16[384,64,128]{2,0,1:T(8,128)(2,1)} copy(bf16[384,64,128]{0,2,1:T(8,128)(2,1)} %bitcast.46) | data formatting | bytes 12582912 | tf_op jit(solution)/shard_map/reshape | solution.py:47
  186.0 11.4 %gather_fusion = bf16[128,384,128]{2,1,0:T(8,128)(2,1)} fusion(bf16[384,64,128]{2,0,1:T(8,128)(2,1)} %copy.21, s32[1024]{0:T(1024)S(1)} %get-tuple-element.15), kind=kCustom, calls=%fused_computation.2 | custom fusion | bytes 25166336 | tf_op jit(solution)/shard_map/jit(_take)/gather | solution.py:47
  197.4 12.6 %select_convert_fusion.1 = bf16[128,128,128]{2,1,0:T(8,128)(2,1)} fusion(pred[128]{0:T(512)(128)(4,1)S(1)} %get-tuple-element.18, bf16[128,384,128]{2,1,0:T(8,128)(2,1)} %gather_fusion, pred[128]{0:T(512)(128)(4,1)S(1)} %get-tuple-element.17, bf16[128,384,128]{2,1,0:T(8,128)(2,1)} %gather_fusion.1, pred[128]{0:T(512)(128)(4,1)S(1)} %get-tuple-element.6), kind=kOutput, calls=%fused_computation.23 | convolution fusion | flops 1627389952 | bytes 29360512 | tf_op jit(solution)/shard_map/tsj,tsk->sjk/dot_general | solution.py:50
  210.0 12.7 %select_convert_fusion = bf16[128,128,128]{2,1,0:T(8,128)(2,1)} fusion(pred[128]{0:T(512)(128)(4,1)S(1)} %get-tuple-element.18, bf16[128,384,128]{2,1,0:T(8,128)(2,1)} %gather_fusion, pred[128]{0:T(512)(128)(4,1)S(1)} %get-tuple-element.17, bf16[128,384,128]{2,1,0:T(8,128)(2,1)} %gather_fusion.2, pred[128]{0:T(512)(128)(4,1)S(1)} %get-tuple-element.6), kind=kOutput, calls=%fused_computation.22 | convolution fusion | flops 1627389952 | bytes 29360512 | tf_op jit(solution)/shard_map/tsj,tsk->sjk/dot_general | solution.py:53
  222.8 132.4 %reduce-scatter.2.cloned.1.call-done = bf16[384,256]{1,0:T(8,128)(2,1)} async-done(((bf16[384,8192]{1,0:T(8,128)(2,1)}), bf16[384,256]{1,0:T(8,128)(2,1)}) %reduce-scatter.2.cloned.1.call-update) | async-done | bytes 196624 | tf_op jit(solution)/shard_map/reduce_scatter | solution.py:46
  355.2 159.9 %all-reduce.3.cloned.1.call-done = (bf16[128,128,128]{2,1,0:T(8,128)(2,1)}, bf16[128,128,128]{2,1,0:T(8,128)(2,1)}) async-done(((bf16[128,128,128]{2,1,0:T(8,128)(2,1)}, bf16[128,128,128]{2,1,0:T(8,128)(2,1)}), (bf16[128,128,128]{2,1,0:T(8,128)(2,1)}, bf16[128,128,128]{2,1,0:T(8,128)(2,1)})) %all-reduce.3.cloned.1.call-update) | async-done | bytes 8388624 | tf_op jit(solution)/shard_map/psum | solution.py:57
  515.1 4.9 copy.42
  520.0 2.0 copy.43
  (15 shorter events, 3.1 us)
Async XLA Ops:
  7.2 170.2 %all-gather.2.cloned.1.call-start = ((), (), s32[]{:S(2)}) async-start(), calls=%async_computation.2 | async-start | bytes 6488064 | tf_op jit(solution)/shard_map/all_gather | solution.py:30
  9.0 346.2 %reduce-scatter.2.cloned.1.call-start = ((), (), s32[]{:S(2)}) async-start(), calls=%async_computation.1 | async-start | bytes 6488064 | tf_op jit(solution)/shard_map/reduce_scatter | solution.py:46
  145.2 369.9 %all-reduce.3.cloned.1.call-start = ((), (), s32[]{:S(2)}) async-start(), calls=%async_computation.3 | async-start | bytes 16777216 | tf_op jit(solution)/shard_map/psum | solution.py:57
  515.1 4.9 copy-start
Sparse Core Ops, SparseCore 0:
  9.6 167.6 all-gather.1
  180.3 174.7 reduce-scatter.1
  358.5 156.5 all-reduce.2
where the time goes:
time: 540 us; the launch traced here: 529 us
  waiting for transfers between devices  307 us (57%)
  local copies, waits for them, and re-layouts  84.4 us (16%)
  other arithmetic  66.1 us (12%)
  matrix products  56.3 us (10%)
  between operations  14.7 us (3%)
    psum x1, waiting for transfers between devices, body(): lax.psum(gate_part.astype(jnp.bfloat16), 'tok').astype(jnp.float32)  160 us
    reduce_scatter x1, waiting for transfers between devices, body(): lax.psum_scatter(terms.astype(jnp.bfloat16), 'wt', scatter_dimension=1, t...  132 us
    scatter-add x2, other arithmetic, densify(): jnp.zeros((owned * col_total, width, width), jnp.bfloat16).at[target]  57.7 us
    transpose x2, local copies, waits for them, and re-layouts, densify(): grid = grid.reshape(owned, col_total, width, width).transpose(0, 2, 1, 3)  24.1 us
    dot_general x1, matrix products, body(): jnp.dot(up_grad, densify(up_kept), preferred_element_type=jnp.float32)  16.4 us
    all_gather x1, waiting for transfers between devices, body(): gathered = lax.all_gather(activations, 'wt', axis=1, tiled=True)  14.9 us
    dot_general x1, matrix products, body(): jnp.dot(gate_grad, densify(gate_kept), preferred_element_type=jnp.float32)  14.5 us
    dot_general x1, matrix products, body(): jnp.einsum('tsj,tsk->sjk', up_sel, feature_sel, preferred_element_type=jn...  12.7 us
  transfers between devices with their start and end apart: 3, of which 3 were waited for; matrix products, arithmetic and copies ran while one was open for 37% of the time, Pallas kernels for 0%

commit v1 on v0

v1 whole, which is shorter than its diff:
```python
import functools

import jax
import jax.numpy as jnp
from jax import lax
from jax.experimental import pallas as pl
from jax.experimental.pallas import tpu as pltpu
from jax.sharding import Mesh
from jax.sharding import PartitionSpec as P

BF = jnp.bfloat16
F32 = jnp.float32
AXES = {"x": ("c", "x"), "z": ("c", "z"), "y": ("yh", "c", "yl")}
SIZES = {"yh": 2, "c": 2, "x": 4, "z": 4, "yl": 2}
TOK = 384
SLOTS = 128
HALF = 64
PAIRS = 36


def shift(value, axis, step):
    pairs = []
    if axis in ("yh", "c", "yl"):
        return lax.ppermute(value, axis, [(0, 1), (1, 0)])
    if axis == "y":
        for yh in range(2):
            for c in range(2):
                for yl in range(2):
                    y = (yh * 2 + yl + (step if c == 0 else -step)) % 4
                    pairs.append(((yh * 2 + c) * 2 + yl, ((y // 2) * 2 + c) * 2 + y % 2))
    else:
        for c in range(2):
            for a in range(4):
                b = (a + (step if c == 0 else -step)) % 4
                pairs.append((c * 4 + a, c * 4 + b))
    return lax.ppermute(value, AXES[axis], pairs)


def add(a, b):
    return (a.astype(F32) + b.astype(F32)).astype(BF)


def terms_kernel(
    tab, order, gate_ref, up_ref, hid_ref, wg_hbm, wu_hbm,
    gut_ref, t0_hbm, t1_hbm, t2_hbm, t3_hbm,
    wbuf, gu, tbuf, wsem, tsem,
):
    copies = [
        pltpu.make_async_copy(wg_hbm, wbuf.at[pl.ds(0, SLOTS), pl.ds(0, 128), :], wsem.at[0]),
        pltpu.make_async_copy(wu_hbm, wbuf.at[pl.ds(0, SLOTS), pl.ds(128, 128), :], wsem.at[1]),
    ]
    for copy in copies:
        copy.start()
    wbuf[SLOTS] = jnp.zeros((256, 128), BF)
    for r in range(4):
        cols = pl.ds(r * 128, 128)
        g = gate_ref[:, cols].astype(F32)
        u = up_ref[:, cols].astype(F32)
        h = hid_ref[:, cols].astype(F32)
        sig = 1.0 / (1.0 + jnp.exp(-g))
        gg = h * u * sig * (1.0 + g * (1.0 - sig))
        ug = h * g * sig
        gu[:, pl.ds(r * 256, 128)] = gg.astype(BF)
        gu[:, pl.ds(r * 256 + 128, 128)] = ug.astype(BF)
        gut_ref[pl.ds(r * 256, 128), :] = gg.T.astype(BF)
        gut_ref[pl.ds(r * 256 + 128, 128), :] = ug.T.astype(BF)
    for copy in copies:
        copy.wait()
    outs = []
    for n, (k, dst) in enumerate(((1, t1_hbm), (2, t2_hbm), (3, t3_hbm), (0, t0_hbm))):

        @pl.loop(0, 8)
        def _(j):
            base = order[k * 8 + j]
            total = jnp.zeros((TOK, 256), F32)
            for r in range(4):
                left = wbuf[tab[r * 64 + base]]
                right = wbuf[tab[r * 64 + base + 1]]
                both = jnp.concatenate([left, right], axis=1)
                total += jnp.dot(gu[:, r * 256 : (r + 1) * 256], both, preferred_element_type=F32)
            tbuf[k * 8 + j] = total.astype(BF)

        out = pltpu.make_async_copy(tbuf.at[pl.ds(k * 8, 8)], dst, tsem.at[n])
        out.start()
        outs.append(out)
    for out in outs:
        out.wait()


def terms(tab, order, gate_pre, up_pre, hidden, wg, wu):
    piece = jax.ShapeDtypeStruct((8, TOK, 256), BF)
    vm = pl.BlockSpec(memory_space=pltpu.VMEM)
    anyspace = pl.BlockSpec(memory_space=pl.ANY)
    return pl.pallas_call(
        terms_kernel,
        out_shape=[jax.ShapeDtypeStruct((1024, TOK), BF)] + [piece] * 4,
        in_specs=[pl.BlockSpec(memory_space=pltpu.SMEM)] * 2 + [vm] * 3 + [anyspace] * 2,
        out_specs=[vm] + [anyspace] * 4,
        scratch_shapes=[
            pltpu.VMEM((SLOTS + 1, 256, 128), BF),
            pltpu.VMEM((TOK, 1024), BF),
            pltpu.VMEM((32, TOK, 256), BF),
            pltpu.SemaphoreType.DMA((2,)),
            pltpu.SemaphoreType.DMA((4,)),
        ],
        compiler_params=pltpu.CompilerParams(vmem_limit_bytes=40 * 1024 * 1024),
        cost_estimate=pl.CostEstimate(flops=2 * TOK * 1024 * 8192, bytes_accessed=18 << 20, transcendentals=TOK * 512),
        name="terms",
    )(tab, order, gate_pre, up_pre, hidden, wg, wu)


def wgrad_kernel(
    lrow, lslot, lact, meta, own_ref, other_ref, *rest,
):
    pieces, out_hbm = rest[:8], rest[8]
    acts, gt, stage, asem, osem = rest[9:]
    copies = [
        pltpu.make_async_copy(piece, acts.at[pl.ds(n * 16, 16)], asem.at[n]) for n, piece in enumerate(pieces)
    ]
    for copy in copies:
        copy.start()
    gt[:, :TOK] = own_ref[...]
    gt[:, TOK:] = other_ref[...]

    @pl.loop(meta[2], SLOTS)
    def _(s):
        stage[s] = jnp.zeros((256, 128), BF)

    for copy in copies:
        copy.wait()
    outs = []
    for h in range(2):

        @pl.loop(0, meta[h])
        def _(p):
            pos = (h * PAIRS + p) * 2
            rows = pl.ds(pl.multiple_of(lrow[pos] * 256, 256), 256)
            left = jnp.concatenate([acts[lact[pos * 2]], acts[lact[pos * 2 + 1]]], axis=0)
            right = jnp.concatenate([acts[lact[pos * 2 + 2]], acts[lact[pos * 2 + 3]]], axis=0)
            both = jnp.concatenate([left, right], axis=1)
            total = jnp.dot(gt[rows, :], both, preferred_element_type=F32).astype(BF)
            stage[lslot[pos]] = total[:, :128]
            stage[lslot[pos + 1]] = total[:, 128:]

        out = pltpu.make_async_copy(
            stage.at[pl.ds(h * HALF, HALF)], out_hbm.at[pl.ds(h * HALF, HALF)], osem.at[h]
        )
        out.start()
        outs.append(out)
    for out in outs:
        out.wait()


def wgrad(lrow, lslot, lact, meta, own, other, pieces):
    vm = pl.BlockSpec(memory_space=pltpu.VMEM)
    anyspace = pl.BlockSpec(memory_space=pl.ANY)
    return pl.pallas_call(
        wgrad_kernel,
        out_shape=jax.ShapeDtypeStruct((SLOTS, 256, 128), BF),
        in_specs=[pl.BlockSpec(memory_space=pltpu.SMEM)] * 4 + [vm] * 2 + [anyspace] * 8,
        out_specs=anyspace,
        scratch_shapes=[
            pltpu.VMEM((128, TOK, 128), BF),
            pltpu.VMEM((1024, 2 * TOK), BF),
            pltpu.VMEM((SLOTS + 1, 256, 128), BF),
            pltpu.SemaphoreType.DMA((8,)),
            pltpu.SemaphoreType.DMA((2,)),
        ],
        compiler_params=pltpu.CompilerParams(vmem_limit_bytes=40 * 1024 * 1024),
        cost_estimate=pl.CostEstimate(flops=2 * 768 * 256 * 128 * 128, bytes_accessed=22 << 20, transcendentals=0),
        name="wgrad",
    )(lrow, lslot, lact, meta, own, other, *pieces)


def tables(block_rows, block_cols, block_count):
    i32 = jnp.int32
    c = lax.axis_index("c")
    x, z = lax.axis_index("x"), lax.axis_index("z")
    yh, yl = lax.axis_index("yh"), lax.axis_index("yl")
    sign = 1 - 2 * c
    slots = jnp.arange(SLOTS, dtype=i32)
    live = slots < block_count[0]
    row = block_rows % 4
    col = block_cols
    key = jnp.where(live, row * 64 + col, -1)
    hit = key[None, :] == jnp.arange(256, dtype=i32)[:, None]
    tab = jnp.min(jnp.where(hit, slots[None, :], SLOTS), axis=1)
    k = jnp.arange(4, dtype=i32)
    xs = (x - sign * k) % 4
    zs = (z - sign * k) % 4
    ys = yl ^ jnp.arange(2, dtype=i32)
    order = (((xs[:, None, None] * 4 + zs[None, :, None]) * 2 + ys[None, None, :]) * 2).reshape(32)
    half = slots // HALF
    same = (row[:, None] == row[None, :]) & (half[:, None] == half[None, :]) & live[None, :]
    rank = jnp.sum(jnp.where(same & (slots[None, :] < slots[:, None]), 1, 0), axis=1)
    count = jnp.sum(
        jnp.where(
            live[None, None, :]
            & (half[None, None, :] == jnp.arange(2, dtype=i32)[:, None, None])
            & (row[None, None, :] == k[None, :, None]),
            1,
            0,
        ),
        axis=2,
    )
    npair = (count + 1) // 2
    first = jnp.sum(jnp.where(k[None, :, None] > k[None, None, :], npair[:, None, :], 0), axis=2)
    mine = (jnp.arange(2, dtype=i32)[None, :, None] == half[:, None, None]) & (
        k[None, None, :] == row[:, None, None]
    )
    start = jnp.sum(jnp.where(mine, first[None], 0), axis=(1, 2))
    place = jnp.where(live, (half * PAIRS + start) * 2 + rank, -1)
    spots = jnp.arange(4 * PAIRS, dtype=i32)
    at = place[None, :] == spots[:, None]
    lslot = jnp.min(jnp.where(at, slots[None, :], SLOTS), axis=1)
    lrow = jnp.sum(jnp.where(at, row[None, :], 0), axis=1)
    lcol = jnp.sum(jnp.where(at, col[None, :], 0), axis=1)
    cx, cz, cy, par = lcol >> 4, (lcol >> 2) & 3, (lcol >> 1) & 1, lcol & 1
    kx = (sign * (x - cx)) % 4
    kz = (sign * (z - cz)) % 4
    lact = []
    for j in range(2):
        ky = (sign * ((yh * 2 + yl) - ((yh ^ j) * 2 + cy))) % 4
        lact.append(jnp.where(par == 0, ky * 16 + kz * 4 + kx, 64 + kz * 16 + ky * 4 + kx))
    lact = jnp.stack(lact, axis=1).reshape(-1)
    meta = jnp.concatenate([jnp.sum(npair, axis=1), block_count]).astype(i32)
    return tab, order, lrow, lslot, lact, meta


def gather_direct(value, axis):
    return [value] + [shift(value, axis, k) for k in (1, 2, 3)]


def gather_ring(value, axis):
    parts = [value]
    for _ in range(3):
        parts.append(shift(parts[-1], axis, 1))
    return parts


def body(
    activations, gate_pre, up_pre, hidden_grad, gate_blocks, up_blocks, block_rows, block_cols, block_count,
):
    tab, order, lrow, lslot, lact, meta = tables(block_rows, block_cols, block_count)
    both = jnp.stack([activations[:, :128], activations[:, 128:]])
    near = gather_direct(both, "x")
    even = jnp.stack([v[0] for v in near])
    odd = jnp.stack([v[1] for v in near])
    gut, t0, t1, t2, t3 = terms(tab, order, gate_pre, up_pre, hidden_grad, gate_blocks, up_blocks)
    other = shift(gut, "yh", 1)
    even = jnp.concatenate(gather_direct(even, "z"))
    odd = jnp.concatenate(gather_direct(odd, "y"))
    pieces = gather_ring(even, "y") + gather_ring(odd, "z")
    moving = shift(t1, "x", 1)
    moving = shift(add(moving, t2), "x", 1)
    moving = shift(add(moving, t3), "x", 1)
    mine = add(moving, t0).reshape(4, 2, TOK, 256)
    moving = shift(mine[1], "z", 1)
    moving = shift(add(moving, mine[2]), "z", 1)
    moving = shift(add(moving, mine[3]), "z", 1)
    keep = moving[0].astype(F32) + mine[0, 0].astype(F32)
    send = add(moving[1], mine[0, 1])
    input_grad = (keep + shift(send, "yl", 1).astype(F32)).astype(BF)
    part = wgrad(lrow, lslot, lact, meta, gut, other, pieces)
    total = add(part, shift(part, "c", 1))
    return input_grad, total[:, :128], total[:, 128:]


def solution(mesh):
    fine = Mesh(mesh.devices.reshape(2, 2, 4, 4, 2), ("yh", "c", "x", "z", "yl"))
    tok, wt = ("yh", "c"), ("x", "z", "yl")
    in_specs = (P(tok, wt),) * 4 + (P(wt, None, None),) * 2 + (P(wt),) * 3
    out_specs = (P(tok, wt), P(wt, None, None), P(wt, None, None))
    return jax.shard_map(body, mesh=fine, in_specs=in_specs, out_specs=out_specs, check_vma=False)
```

time: 540 us -> 264 us (0.49); the launches traced: 529 us -> 265 us
  waiting for transfers between devices: 307 us -> 165 us
  local copies, waits for them, and re-layouts: 84.4 us -> 20.2 us
  other arithmetic: 66.1 us -> 7.5 us
  matrix products: 56.3 us -> 0 us
  Pallas kernels: 0 us -> 37 us
  starting transfers between devices: 0.12 us -> 32.8 us
  between operations: 14.7 us -> 1.59 us
    ppermute x0 -> x24, waiting for transfers between devices: none -> 165 us  [the longest x21 160 us: shift(): return lax.ppermute(value, AXES[axis], pairs)]
    psum x1 -> x0, waiting for transfers between devices: 160 us -> none  [body(): lax.psum(gate_part.astype(jnp.bfloat16), 'tok').astype(jnp.float32)]
    reduce_scatter x1 -> x0, waiting for transfers between devices: 132 us -> none  [body(): lax.psum_scatter(terms.astype(jnp.bfloat16), 'wt', scatter_dimension=1, t...]
    scatter-add x2 -> x0, other arithmetic: 57.7 us -> none  [densify(): jnp.zeros((owned * col_total, width, width), jnp.bfloat16).at[target]]
    dot_general x4 -> x0, matrix products: 56.3 us -> none  [the longest x1 16.4 us: body(): jnp.dot(up_grad, densify(up_kept), preferred_element_type=jnp.float32)]
    pallas_call x0 -> x2, Pallas kernels: none -> 37 us  [the longest x1 19.6 us: wgrad(): pl.pallas_call(wgrad_kernel, out_shape=jax.ShapeDtypeStruct((SLOTS, 256,...]
    ppermute x0 -> x24, starting transfers between devices: none -> 32.8 us  [the longest x21 30.2 us: shift(): return lax.ppermute(value, AXES[axis], pairs)]
    gather x3 -> x0, local copies, waits for them, and re-layouts: 28.1 us -> none  [the longest x1 11.4 us: body(): jnp.take(gathered.reshape(tok_rows, col_total, width), block_cols, axis=1)]
  transfers between devices with their start and end apart: 3 -> 24, of which waited for: 3 -> 14; matrix products, arithmetic and copies ran while one was open for 37% -> 4% of each run, Pallas kernels for 0% -> 7%
where the time goes in v1:
time: 264 us; the launch traced here: 265 us
  waiting for transfers between devices  165 us (62%)
  Pallas kernels  37 us (14%)
  starting transfers between devices  32.8 us (12%)
  local copies, waits for them, and re-layouts  20.2 us (8%)
  other arithmetic  7.5 us (3%)
    ppermute x21, waiting for transfers between devices, shift(): return lax.ppermute(value, AXES[axis], pairs)  160 us
    ppermute x21, starting transfers between devices, shift(): return lax.ppermute(value, AXES[axis], pairs)  30.2 us
    pallas_call x1, Pallas kernels, wgrad(): pl.pallas_call(wgrad_kernel, out_shape=jax.ShapeDtypeStruct((SLOTS, 256,...  19.6 us
    pallas_call x1, Pallas kernels, terms(): pl.pallas_call(terms_kernel, out_shape=[jax.ShapeDtypeStruct((1024, TOK),...  17.4 us
    unnamed x29, local copies, waits for them, and re-layouts  11.2 us
    ppermute x3, waiting for transfers between devices, shift(): return lax.ppermute(value, axis, [(0, 1), (1, 0)])  5.66 us
  transfers between devices with their start and end apart: 24, of which 14 were waited for; matrix products, arithmetic and copies ran while one was open for 4% of the time, Pallas kernels for 7%

profile of v1, /device:TPU:0, one launch (start us, length us, event | category | flops | bytes accessed | tf_op | source)
XLA Modules:
  0.0 264.5 jit_solution(14047808708177297661)
XLA Ops:
  1.6 2.9 %collective-permute-start.10 = (bf16[2,384,128]{2,1,0:T(8,128)(2,1)S(1)}, bf16[2,384,128]{2,1,0:T(8,128)(2,1)S(1)}, u32[]{:S(2)}, u32[]{:S(2)}) collective-permute-start(bf16[2,384,128]{2,1,0:T(8,128)(2,1)S(1)} %pad_maximum_fusion.2), channel_id=1, source_target_pairs={{0,24},{8,0},{16,8},{24,16},{32,40},{40,48},{48,56},{56,32},{1,25}... | collective-permute-start | bytes 589832 | tf_op jit(solution)/shard_map/ppermute | solution.py:36
  7.9 7.0 %collective-permute-done.8 = bf16[2,384,128]{2,1,0:T(8,128)(2,1)S(1)} collective-permute-done((bf16[2,384,128]{2,1,0:T(8,128)(2,1)S(1)}, bf16[2,384,128]{2,1,0:T(8,128)(2,1)S(1)}, u32[]{:S(2)}, u32[]{:S(2)}) %collective-permute-start.8) | collective-permute-done | bytes 196640 | tf_op jit(solution)/shard_map/ppermute | solution.py:36
  19.1 3.6 %collective-permute-start.12 = (bf16[4,384,128]{2,1,0:T(8,128)(2,1)S(1)}, bf16[4,384,128]{2,1,0:T(8,128)(2,1)S(1)}, u32[]{:S(2)}, u32[]{:S(2)}) collective-permute-start(bf16[4,384,128]{2,1,0:T(8,128)(2,1)S(1)} %pad_maximum_fusion), channel_id=1, source_target_pairs={{0,4},{2,6},{4,0},{6,2},{32,36},{34,38},{36,32},{38,34},{1,5},{3,7... | collective-permute-start | bytes 1179656 | tf_op jit(solution)/shard_map/ppermute | solution.py:36
  26.0 3.0 %collective-permute-start.18 = (bf16[4,384,128]{2,1,0:T(8,128)(2,1)S(1)}, bf16[4,384,128]{2,1,0:T(8,128)(2,1)S(1)}, u32[]{:S(2)}, u32[]{:S(2)}) collective-permute-start(bf16[4,384,128]{2,1,0:T(8,128)(2,1)S(1)} %pad_maximum_fusion.1), channel_id=1, source_target_pairs={{0,64},{1,65},{32,96},{33,97},{64,0},{65,1},{96,32},{97,33},{2,66}... | collective-permute-start | bytes 1179656 | tf_op jit(solution)/shard_map/ppermute | solution.py:36
  29.0 6.9 %collective-permute-done.11 = bf16[4,384,128]{2,1,0:T(8,128)(2,1)S(1)} collective-permute-done((bf16[4,384,128]{2,1,0:T(8,128)(2,1)S(1)}, bf16[4,384,128]{2,1,0:T(8,128)(2,1)S(1)}, u32[]{:S(2)}, u32[]{:S(2)}) %collective-permute-start.11) | collective-permute-done | bytes 393248 | tf_op jit(solution)/shard_map/ppermute | solution.py:36
  35.9 3.0 %collective-permute-start.19 = (bf16[4,384,128]{2,1,0:T(8,128)(2,1)S(1)}, bf16[4,384,128]{2,1,0:T(8,128)(2,1)S(1)}, u32[]{:S(2)}, u32[]{:S(2)}) collective-permute-start(bf16[4,384,128]{2,1,0:T(8,128)(2,1)S(1)} %pad_maximum_fusion.1), channel_id=1, source_target_pairs={{0,65},{1,0},{32,33},{33,96},{64,1},{65,64},{96,97},{97,32},{2,67}... | collective-permute-start | bytes 1179656 | tf_op jit(solution)/shard_map/ppermute | solution.py:36
  46.8 2.3 collective-permute-start.20
  49.6 2.2 copy-done.2
  53.7 17.4 %terms.1 = (bf16[1024,384]{1,0:T(8,128)(2,1)}, bf16[8,384,256]{2,1,0:T(8,128)(2,1)S(1)}, bf16[8,384,256]{2,1,0:T(8,128)(2,1)S(1)}, bf16[8,384,256]{2,1,0:T(8,128)(2,1)S(1)}, bf16[8,384,256]{2,1,0:T(8,128)(2,1)S(1)}) custom-call(s32[256]{0:T(256)S(1)} %select_reduce_fusion.tab, s32[32]{0:T(128)S(1)} %mul.220.order, bf16[384,512]{1,0:T(8,128)(2,1)S(1)} %copy-done.5, ...), custom_call_target="tpu_custom_call" | custom-call | flops 6442450944 | bytes 18874368 | tf_op jit(solution)/shard_map/terms/pallas_call | solution.py:94
  73.4 2.4 collective-permute-start.7
  75.8 2.2 collective-permute-start.15
  78.1 4.3 %collective-permute-start.21 = (bf16[16,384,128]{2,1,0:T(8,128)(2,1)}, bf16[16,384,128]{2,1,0:T(8,128)(2,1)}, u32[]{:S(2)}, u32[]{:S(2)}) collective-permute-start(bf16[16,384,128]{2,1,0:T(8,128)(2,1)} %collective-permute-done.20.rest_5_), channel_id=1, source_target_pairs={{0,2},{2,4},{4,6},{6,0},{32,38},{34,32},{36,34},{38,36},{1,3},{3,5... | collective-permute-start | bytes 4718600 | tf_op jit(solution)/shard_map/ppermute | solution.py:36
  83.0 27.7 %collective-permute-done.15.rest_2_ = bf16[16,384,128]{2,1,0:T(8,128)(2,1)} collective-permute-done((bf16[16,384,128]{2,1,0:T(8,128)(2,1)}, bf16[16,384,128]{2,1,0:T(8,128)(2,1)}, u32[]{:S(2)}, u32[]{:S(2)}) %collective-permute-start.15) | collective-permute-done | bytes 1572896 | tf_op jit(solution)/shard_map/ppermute | solution.py:36
  111.8 20.8 %collective-permute-done.16.rest_3_ = bf16[16,384,128]{2,1,0:T(8,128)(2,1)} collective-permute-done((bf16[16,384,128]{2,1,0:T(8,128)(2,1)}, bf16[16,384,128]{2,1,0:T(8,128)(2,1)}, u32[]{:S(2)}, u32[]{:S(2)}) %collective-permute-start.16) | collective-permute-done | bytes 1572896 | tf_op jit(solution)/shard_map/ppermute | solution.py:36
  133.0 19.6 %wgrad.1 = bf16[128,256,128]{2,1,0:T(8,128)(2,1)} custom-call(s32[144]{0:T(256)S(1)} %get-tuple-element.15.lrow, s32[144]{0:T(256)S(1)} %get-tuple-element.14.lslot, s32[288]{0:T(512)S(1)} %reshape.594.lact, s32[3]{0:T(128)S(1)} %pad_add_fusion.1.meta, bf16[1024,384]{1,0:T(8,128)(2,1)} %get-tuple-element.12.own_ref, ...), custom_call_target="tpu_custom_call" | custom-call | flops 6442450944 | bytes 23068672 | tf_op jit(solution)/shard_map/wgrad/pallas_call | solution.py:157
  152.8 21.6 %collective-permute-done = bf16[8,384,256]{2,1,0:T(8,128)(2,1)S(1)} collective-permute-done((bf16[8,384,256]{2,1,0:T(8,128)(2,1)S(1)}, bf16[8,384,256]{2,1,0:T(8,128)(2,1)S(1)}, u32[]{:S(2)}, u32[]{:S(2)}) %collective-permute-start) | collective-permute-done | bytes 1572896 | tf_op jit(solution)/shard_map/ppermute | solution.py:36
  174.9 21.6 %collective-permute-done.1 = bf16[8,384,256]{2,1,0:T(8,128)(2,1)S(1)} collective-permute-done((bf16[8,384,256]{2,1,0:T(8,128)(2,1)S(1)}, bf16[8,384,256]{2,1,0:T(8,128)(2,1)S(1)}, u32[]{:S(2)}, u32[]{:S(2)}) %collective-permute-start.1) | collective-permute-done | bytes 1572896 | tf_op jit(solution)/shard_map/ppermute | solution.py:36
  197.3 21.6 %collective-permute-done.2 = bf16[8,384,256]{2,1,0:T(8,128)(2,1)S(1)} collective-permute-done((bf16[8,384,256]{2,1,0:T(8,128)(2,1)S(1)}, bf16[8,384,256]{2,1,0:T(8,128)(2,1)S(1)}, u32[]{:S(2)}, u32[]{:S(2)}) %collective-permute-start.2) | collective-permute-done | bytes 1572896 | tf_op jit(solution)/shard_map/ppermute | solution.py:36
  219.4 12.6 %collective-permute-done.3 = bf16[2,384,256]{2,1,0:T(8,128)(2,1)S(1)} collective-permute-done((bf16[2,384,256]{2,1,0:T(8,128)(2,1)S(1)}, bf16[2,384,256]{2,1,0:T(8,128)(2,1)S(1)}, u32[]{:S(2)}, u32[]{:S(2)}) %collective-permute-start.3) | collective-permute-done | bytes 393248 | tf_op jit(solution)/shard_map/ppermute | solution.py:36
  232.2 9.0 %collective-permute-done.4 = bf16[2,384,256]{2,1,0:T(8,128)(2,1)S(1)} collective-permute-done((bf16[2,384,256]{2,1,0:T(8,128)(2,1)S(1)}, bf16[2,384,256]{2,1,0:T(8,128)(2,1)S(1)}, u32[]{:S(2)}, u32[]{:S(2)}) %collective-permute-start.4) | collective-permute-done | bytes 393248 | tf_op jit(solution)/shard_map/ppermute | solution.py:36
  241.4 9.0 %collective-permute-done.5 = bf16[2,384,256]{2,1,0:T(8,128)(2,1)S(1)} collective-permute-done((bf16[2,384,256]{2,1,0:T(8,128)(2,1)S(1)}, bf16[2,384,256]{2,1,0:T(8,128)(2,1)S(1)}, u32[]{:S(2)}, u32[]{:S(2)}) %collective-permute-start.5) | collective-permute-done | bytes 393248 | tf_op jit(solution)/shard_map/ppermute | solution.py:36
  250.5 5.7 %collective-permute-done.6 = bf16[384,256]{1,0:T(8,128)(2,1)S(1)} collective-permute-done((bf16[384,256]{1,0:T(8,128)(2,1)S(1)}, bf16[384,256]{1,0:T(8,128)(2,1)S(1)}, u32[]{:S(2)}, u32[]{:S(2)}) %collective-permute-start.6) | collective-permute-done | bytes 196640 | tf_op jit(solution)/shard_map/ppermute | solution.py:24
  256.9 3.7 %add_convert_fusion = bf16[128,256,128]{2,1,0:T(8,128)(2,1)S(1)} fusion(bf16[128,256,128]{2,1,0:T(8,128)(2,1)S(1)} %collective-permute-done.23, bf16[128,256,128]{2,1,0:T(8,128)(2,1)S(1)} %bitcast.38), kind=kLoop, calls=%fused_computation | loop fusion | flops 16777216 | bytes 25165824 | tf_op jit(solution)/shard_map/convert_element_type | solution.py:40
  260.7 3.9 %fusion.13 = (bf16[128,128,128]{2,1,0:T(8,128)(2,1)}, bf16[128,128,128]{2,1,0:T(8,128)(2,1)}) fusion(bf16[128,256,128]{2,1,0:T(8,128)(2,1)S(1)} %add_convert_fusion), kind=kLoop, calls=%fused_computation.107 | loop fusion | bytes 16777216 | tf_op jit(solution)/shard_map/slice | solution.py:266
  (103 shorter events, 29.1 us)
Async XLA Ops:
  1.6 14.7 %collective-permute-start.10 = (bf16[2,384,128]{2,1,0:T(8,128)(2,1)S(1)}, bf16[2,384,128]{2,1,0:T(8,128)(2,1)S(1)}, u32[]{:S(2)}, u32[]{:S(2)}) collective-permute-start(bf16[2,384,128]{2,1,0:T(8,128)(2,1)S(1)} %pad_maximum_fusion.2), channel_id=1, source_target_pairs={{0,24},{8,0},{16,8},{24,16},{32,40},{40,48},{48,56},{56,32},{1,25}... | collective-permute-start | bytes 589832 | tf_op jit(solution)/shard_map/ppermute | solution.py:36
  4.5 11.0 %collective-permute-start.9 = (bf16[2,384,128]{2,1,0:T(8,128)(2,1)S(1)}, bf16[2,384,128]{2,1,0:T(8,128)(2,1)S(1)}, u32[]{:S(2)}, u32[]{:S(2)}) collective-permute-start(bf16[2,384,128]{2,1,0:T(8,128)(2,1)S(1)} %pad_maximum_fusion.2), channel_id=1, source_target_pairs={{0,16},{8,24},{16,0},{24,8},{32,48},{40,56},{48,32},{56,40},{1,17}... | collective-permute-start | bytes 589832 | tf_op jit(solution)/shard_map/ppermute | solution.py:36
  5.3 9.5 %collective-permute-start.8 = (bf16[2,384,128]{2,1,0:T(8,128)(2,1)S(1)}, bf16[2,384,128]{2,1,0:T(8,128)(2,1)S(1)}, u32[]{:S(2)}, u32[]{:S(2)}) collective-permute-start(bf16[2,384,128]{2,1,0:T(8,128)(2,1)S(1)} %pad_maximum_fusion.2), channel_id=1, source_target_pairs={{0,8},{8,16},{16,24},{24,0},{32,56},{40,32},{48,40},{56,48},{1,9},... | collective-permute-start | bytes 589832 | tf_op jit(solution)/shard_map/ppermute | solution.py:36
  17.1 18.8 %collective-permute-start.11 = (bf16[4,384,128]{2,1,0:T(8,128)(2,1)S(1)}, bf16[4,384,128]{2,1,0:T(8,128)(2,1)S(1)}, u32[]{:S(2)}, u32[]{:S(2)}) collective-permute-start(bf16[4,384,128]{2,1,0:T(8,128)(2,1)S(1)} %pad_maximum_fusion), channel_id=1, source_target_pairs={{0,2},{2,4},{4,6},{6,0},{32,38},{34,32},{36,34},{38,36},{1,3},{3,5... | collective-permute-start | bytes 1179656 | tf_op jit(solution)/shard_map/ppermute | solution.py:36
  19.1 21.9 %collective-permute-start.12 = (bf16[4,384,128]{2,1,0:T(8,128)(2,1)S(1)}, bf16[4,384,128]{2,1,0:T(8,128)(2,1)S(1)}, u32[]{:S(2)}, u32[]{:S(2)}) collective-permute-start(bf16[4,384,128]{2,1,0:T(8,128)(2,1)S(1)} %pad_maximum_fusion), channel_id=1, source_target_pairs={{0,4},{2,6},{4,0},{6,2},{32,36},{34,38},{36,32},{38,34},{1,5},{3,7... | collective-permute-start | bytes 1179656 | tf_op jit(solution)/shard_map/ppermute | solution.py:36
  22.7 19.1 %collective-permute-start.13 = (bf16[4,384,128]{2,1,0:T(8,128)(2,1)S(1)}, bf16[4,384,128]{2,1,0:T(8,128)(2,1)S(1)}, u32[]{:S(2)}, u32[]{:S(2)}) collective-permute-start(bf16[4,384,128]{2,1,0:T(8,128)(2,1)S(1)} %pad_maximum_fusion), channel_id=1, source_target_pairs={{0,6},{2,0},{4,2},{6,4},{32,34},{34,36},{36,38},{38,32},{1,7},{3,1... | collective-permute-start | bytes 1179656 | tf_op jit(solution)/shard_map/ppermute | solution.py:36
  23.7 20.4 %collective-permute-start.17 = (bf16[4,384,128]{2,1,0:T(8,128)(2,1)S(1)}, bf16[4,384,128]{2,1,0:T(8,128)(2,1)S(1)}, u32[]{:S(2)}, u32[]{:S(2)}) collective-permute-start(bf16[4,384,128]{2,1,0:T(8,128)(2,1)S(1)} %pad_maximum_fusion.1), channel_id=1, source_target_pairs={{0,1},{1,64},{32,97},{33,32},{64,65},{65,0},{96,33},{97,96},{2,3},... | collective-permute-start | bytes 1179656 | tf_op jit(solution)/shard_map/ppermute | solution.py:36
  26.0 18.9 %collective-permute-start.18 = (bf16[4,384,128]{2,1,0:T(8,128)(2,1)S(1)}, bf16[4,384,128]{2,1,0:T(8,128)(2,1)S(1)}, u32[]{:S(2)}, u32[]{:S(2)}) collective-permute-start(bf16[4,384,128]{2,1,0:T(8,128)(2,1)S(1)} %pad_maximum_fusion.1), channel_id=1, source_target_pairs={{0,64},{1,65},{32,96},{33,97},{64,0},{65,1},{96,32},{97,33},{2,66}... | collective-permute-start | bytes 1179656 | tf_op jit(solution)/shard_map/ppermute | solution.py:36
  35.9 10.1 %collective-permute-start.19 = (bf16[4,384,128]{2,1,0:T(8,128)(2,1)S(1)}, bf16[4,384,128]{2,1,0:T(8,128)(2,1)S(1)}, u32[]{:S(2)}, u32[]{:S(2)}) collective-permute-start(bf16[4,384,128]{2,1,0:T(8,128)(2,1)S(1)} %pad_maximum_fusion.1), channel_id=1, source_target_pairs={{0,65},{1,0},{32,33},{33,96},{64,1},{65,64},{96,97},{97,32},{2,67}... | collective-permute-start | bytes 1179656 | tf_op jit(solution)/shard_map/ppermute | solution.py:36
  42.5 33.3 %collective-permute-start.14 = (bf16[16,384,128]{2,1,0:T(8,128)(2,1)}, bf16[16,384,128]{2,1,0:T(8,128)(2,1)}, u32[]{:S(2)}, u32[]{:S(2)}) collective-permute-start(bf16[16,384,128]{2,1,0:T(8,128)(2,1)} %constant_dynamic-update-slice_fusion.rest_0_), channel_id=1, source_target_pairs={{0,1},{1,64},{32,97},{33,32},{64,65},{65,0},{96,33},{97,96},{2,3},... | collective-permute-start | bytes 4718600 | tf_op jit(solution)/shard_map/ppermute | solution.py:36
  46.8 31.2 %collective-permute-start.20 = (bf16[16,384,128]{2,1,0:T(8,128)(2,1)}, bf16[16,384,128]{2,1,0:T(8,128)(2,1)}, u32[]{:S(2)}, u32[]{:S(2)}) collective-permute-start(bf16[16,384,128]{2,1,0:T(8,128)(2,1)} %constant_dynamic-update-slice_fusion.7.rest_4_), channel_id=1, source_target_pairs={{0,2},{2,4},{4,6},{6,0},{32,38},{34,32},{36,34},{38,36},{1,3},{3,5... | collective-permute-start | bytes 4718600 | tf_op jit(solution)/shard_map/ppermute | solution.py:36
  73.4 38.4 %collective-permute-start.7 = (bf16[1024,384]{1,0:T(8,128)(2,1)}, bf16[1024,384]{1,0:T(8,128)(2,1)}, u32[]{:S(2)}, u32[]{:S(2)}) collective-permute-start(bf16[1024,384]{1,0:T(8,128)(2,1)} %get-tuple-element.12.own_ref), channel_id=1, source_target_pairs={{0,64},{64,0},{1,65},{65,1},{2,66},{66,2},{3,67},{67,3},{4,68},{68... | collective-permute-start | bytes 2359304 | tf_op jit(solution)/shard_map/ppermute | solution.py:24
  75.8 34.9 %collective-permute-start.15 = (bf16[16,384,128]{2,1,0:T(8,128)(2,1)}, bf16[16,384,128]{2,1,0:T(8,128)(2,1)}, u32[]{:S(2)}, u32[]{:S(2)}) collective-permute-start(bf16[16,384,128]{2,1,0:T(8,128)(2,1)} %collective-permute-done.14.rest_1_), channel_id=1, source_target_pairs={{0,1},{1,64},{32,97},{33,32},{64,65},{65,0},{96,33},{97,96},{2,3},... | collective-permute-start | bytes 4718600 | tf_op jit(solution)/shard_map/ppermute | solution.py:36
  78.1 33.0 %collective-permute-start.21 = (bf16[16,384,128]{2,1,0:T(8,128)(2,1)}, bf16[16,384,128]{2,1,0:T(8,128)(2,1)}, u32[]{:S(2)}, u32[]{:S(2)}) collective-permute-start(bf16[16,384,128]{2,1,0:T(8,128)(2,1)} %collective-permute-done.20.rest_5_), channel_id=1, source_target_pairs={{0,2},{2,4},{4,6},{6,0},{32,38},{34,32},{36,34},{38,36},{1,3},{3,5... | collective-permute-start | bytes 4718600 | tf_op jit(solution)/shard_map/ppermute | solution.py:36
  110.7 21.9 %collective-permute-start.16 = (bf16[16,384,128]{2,1,0:T(8,128)(2,1)}, bf16[16,384,128]{2,1,0:T(8,128)(2,1)}, u32[]{:S(2)}, u32[]{:S(2)}) collective-permute-start(bf16[16,384,128]{2,1,0:T(8,128)(2,1)} %collective-permute-done.15.rest_2_), channel_id=1, source_target_pairs={{0,1},{1,64},{32,97},{33,32},{64,65},{65,0},{96,33},{97,96},{2,3},... | collective-permute-start | bytes 4718600 | tf_op jit(solution)/shard_map/ppermute | solution.py:36
  111.1 21.9 %collective-permute-start.22 = (bf16[16,384,128]{2,1,0:T(8,128)(2,1)}, bf16[16,384,128]{2,1,0:T(8,128)(2,1)}, u32[]{:S(2)}, u32[]{:S(2)}) collective-permute-start(bf16[16,384,128]{2,1,0:T(8,128)(2,1)} %collective-permute-done.21.rest_6_), channel_id=1, source_target_pairs={{0,2},{2,4},{4,6},{6,0},{32,38},{34,32},{36,34},{38,36},{1,3},{3,5... | collective-permute-start | bytes 4718600 | tf_op jit(solution)/shard_map/ppermute | solution.py:36
  152.6 104.3 %collective-permute-start.23 = (bf16[128,256,128]{2,1,0:T(8,128)(2,1)}, bf16[128,256,128]{2,1,0:T(8,128)(2,1)S(1)}, u32[]{:S(2)}, u32[]{:S(2)}) collective-permute-start(bf16[128,256,128]{2,1,0:T(8,128)(2,1)} %wgrad.1), channel_id=1, source_target_pairs={{0,32},{32,0},{1,33},{33,1},{2,34},{34,2},{3,35},{35,3},{4,36},{36... | collective-permute-start | bytes 25165832 | tf_op jit(solution)/shard_map/ppermute | solution.py:24
  152.7 21.7 %collective-permute-start = (bf16[8,384,256]{2,1,0:T(8,128)(2,1)S(1)}, bf16[8,384,256]{2,1,0:T(8,128)(2,1)S(1)}, u32[]{:S(2)}, u32[]{:S(2)}) collective-permute-start(bf16[8,384,256]{2,1,0:T(8,128)(2,1)S(1)} %copy-done.4), channel_id=1, source_target_pairs={{0,8},{8,16},{16,24},{24,0},{32,56},{40,32},{48,40},{56,48},{1,9},... | collective-permute-start | bytes 4718600 | tf_op jit(solution)/shard_map/ppermute | solution.py:36
  174.9 21.7 %collective-permute-start.1 = (bf16[8,384,256]{2,1,0:T(8,128)(2,1)S(1)}, bf16[8,384,256]{2,1,0:T(8,128)(2,1)S(1)}, u32[]{:S(2)}, u32[]{:S(2)}) collective-permute-start(bf16[8,384,256]{2,1,0:T(8,128)(2,1)S(1)} %add_convert_fusion.3), channel_id=1, source_target_pairs={{0,8},{8,16},{16,24},{24,0},{32,56},{40,32},{48,40},{56,48},{1,9},... | collective-permute-start | bytes 4718600 | tf_op jit(solution)/shard_map/ppermute | solution.py:36
  197.0 21.9 %collective-permute-start.2 = (bf16[8,384,256]{2,1,0:T(8,128)(2,1)S(1)}, bf16[8,384,256]{2,1,0:T(8,128)(2,1)S(1)}, u32[]{:S(2)}, u32[]{:S(2)}) collective-permute-start(bf16[8,384,256]{2,1,0:T(8,128)(2,1)S(1)} %add_convert_fusion.2), channel_id=1, source_target_pairs={{0,8},{8,16},{16,24},{24,0},{32,56},{40,32},{48,40},{56,48},{1,9},... | collective-permute-start | bytes 4718600 | tf_op jit(solution)/shard_map/ppermute | solution.py:36
  219.3 12.7 %collective-permute-start.3 = (bf16[2,384,256]{2,1,0:T(8,128)(2,1)S(1)}, bf16[2,384,256]{2,1,0:T(8,128)(2,1)S(1)}, u32[]{:S(2)}, u32[]{:S(2)}) collective-permute-start(bf16[2,384,256]{2,1,0:T(8,128)(2,1)S(1)} %slice.71), channel_id=1, source_target_pairs={{0,2},{2,4},{4,6},{6,0},{32,38},{34,32},{36,34},{38,36},{1,3},{3,5... | collective-permute-start | bytes 1179656 | tf_op jit(solution)/shard_map/ppermute | solution.py:36
  232.1 9.1 %collective-permute-start.4 = (bf16[2,384,256]{2,1,0:T(8,128)(2,1)S(1)}, bf16[2,384,256]{2,1,0:T(8,128)(2,1)S(1)}, u32[]{:S(2)}, u32[]{:S(2)}) collective-permute-start(bf16[2,384,256]{2,1,0:T(8,128)(2,1)S(1)} %add_convert_fusion.5), channel_id=1, source_target_pairs={{0,2},{2,4},{4,6},{6,0},{32,38},{34,32},{36,34},{38,36},{1,3},{3,5... | collective-permute-start | bytes 1179656 | tf_op jit(solution)/shard_map/ppermute | solution.py:36
  241.3 9.1 %collective-permute-start.5 = (bf16[2,384,256]{2,1,0:T(8,128)(2,1)S(1)}, bf16[2,384,256]{2,1,0:T(8,128)(2,1)S(1)}, u32[]{:S(2)}, u32[]{:S(2)}) collective-permute-start(bf16[2,384,256]{2,1,0:T(8,128)(2,1)S(1)} %add_convert_fusion.4), channel_id=1, source_target_pairs={{0,2},{2,4},{4,6},{6,0},{32,38},{34,32},{36,34},{38,36},{1,3},{3,5... | collective-permute-start | bytes 1179656 | tf_op jit(solution)/shard_map/ppermute | solution.py:36
  250.4 5.7 %collective-permute-start.6 = (bf16[384,256]{1,0:T(8,128)(2,1)S(1)}, bf16[384,256]{1,0:T(8,128)(2,1)S(1)}, u32[]{:S(2)}, u32[]{:S(2)}) collective-permute-start(bf16[384,256]{1,0:T(8,128)(2,1)S(1)} %fusion), channel_id=1, source_target_pairs={{0,1},{1,0},{2,3},{3,2},{4,5},{5,4},{6,7},{7,6},{8,9},{9,8},{10,11... | collective-permute-start | bytes 589832 | tf_op jit(solution)/shard_map/ppermute | solution.py:24
  (12 other events, 233.5 us)

commit v2 on v1

--- a/solution.py
+++ b/solution.py
@@ -40,11 +40,7 @@
     return (a.astype(F32) + b.astype(F32)).astype(BF)
 
 
-def terms_kernel(
-    tab, order, gate_ref, up_ref, hid_ref, wg_hbm, wu_hbm,
-    gut_ref, t0_hbm, t1_hbm, t2_hbm, t3_hbm,
-    wbuf, gu, tbuf, wsem, tsem,
-):
+def load_blocks(wg_hbm, wu_hbm, wbuf, wsem):
     copies = [
         pltpu.make_async_copy(wg_hbm, wbuf.at[pl.ds(0, SLOTS), pl.ds(0, 128), :], wsem.at[0]),
         pltpu.make_async_copy(wu_hbm, wbuf.at[pl.ds(0, SLOTS), pl.ds(128, 128), :], wsem.at[1]),
@@ -52,6 +48,24 @@
     for copy in copies:
         copy.start()
     wbuf[SLOTS] = jnp.zeros((256, 128), BF)
+    return copies
+
+
+def term_chunk(k, tab, order, gu, wbuf, out):
+    @pl.loop(0, 8)
+    def _(j):
+        base = order[k * 8 + j]
+        total = jnp.zeros((TOK, 256), F32)
+        for r in range(4):
+            left = wbuf[tab[r * 64 + base]]
+            right = wbuf[tab[r * 64 + base + 1]]
+            both = jnp.concatenate([left, right], axis=1)
+            total += jnp.dot(gu[:, r * 256 : (r + 1) * 256], both, preferred_element_type=F32)
+        out[j] = total.astype(BF)
+
+
+def first_kernel(tab, order, gate_ref, up_ref, hid_ref, wg_hbm, wu_hbm, gu, gut_ref, t1, wbuf, wsem):
+    copies = load_blocks(wg_hbm, wu_hbm, wbuf, wsem)
     for r in range(4):
         cols = pl.ds(r * 128, 128)
         g = gate_ref[:, cols].astype(F32)
@@ -66,47 +80,47 @@
         gut_ref[pl.ds(r * 256 + 128, 128), :] = ug.T.astype(BF)
     for copy in copies:
         copy.wait()
-    outs = []
-    for n, (k, dst) in enumerate(((1, t1_hbm), (2, t2_hbm), (3, t3_hbm), (0, t0_hbm))):
-
-        @pl.loop(0, 8)
-        def _(j):
-            base = order[k * 8 + j]
-            total = jnp.zeros((TOK, 256), F32)
-            for r in range(4):
-                left = wbuf[tab[r * 64 + base]]
-                right = wbuf[tab[r * 64 + base + 1]]
-                both = jnp.concatenate([left, right], axis=1)
-                total += jnp.dot(gu[:, r * 256 : (r + 1) * 256], both, preferred_element_type=F32)
-            tbuf[k * 8 + j] = total.astype(BF)
-
-        out = pltpu.make_async_copy(tbuf.at[pl.ds(k * 8, 8)], dst, tsem.at[n])
-        out.start()
-        outs.append(out)
-    for out in outs:
-        out.wait()
-
-
-def terms(tab, order, gate_pre, up_pre, hidden, wg, wu):
-    piece = jax.ShapeDtypeStruct((8, TOK, 256), BF)
-    vm = pl.BlockSpec(memory_space=pltpu.VMEM)
-    anyspace = pl.BlockSpec(memory_space=pl.ANY)
+    term_chunk(1, tab, order, gu, wbuf, t1)
+
+
+def rest_kernel(tab, order, gu, wg_hbm, wu_hbm, t2, t3, t0, wbuf, wsem):
+    for copy in load_blocks(wg_hbm, wu_hbm, wbuf, wsem):
+        copy.wait()
+    for k, out in ((2, t2), (3, t3), (0, t0)):
+        term_chunk(k, tab, order, gu, wbuf, out)
+
+
+PIECE = jax.ShapeDtypeStruct((8, TOK, 256), BF)
+VM = pl.BlockSpec(memory_space=pltpu.VMEM)
+SM = pl.BlockSpec(memory_space=pltpu.SMEM)
+ANY = pl.BlockSpec(memory_space=pl.ANY)
+BLOCK_SCRATCH = [pltpu.VMEM((SLOTS + 1, 256, 128), BF), pltpu.SemaphoreType.DMA((2,))]
+
+
+def first_terms(tab, order, gate_pre, up_pre, hidden, wg, wu):
     return pl.pallas_call(
-        terms_kernel,
-        out_shape=[jax.ShapeDtypeStruct((1024, TOK), BF)] + [piece] * 4,
-        in_specs=[pl.BlockSpec(memory_space=pltpu.SMEM)] * 2 + [vm] * 3 + [anyspace] * 2,
-        out_specs=[vm] + [anyspace] * 4,
-        scratch_shapes=[
-            pltpu.VMEM((SLOTS + 1, 256, 128), BF),
-            pltpu.VMEM((TOK, 1024), BF),
-            pltpu.VMEM((32, TOK, 256), BF),
-            pltpu.SemaphoreType.DMA((2,)),
-            pltpu.SemaphoreType.DMA((4,)),
-        ],
+        first_kernel,
+        out_shape=[jax.ShapeDtypeStruct((TOK, 1024), BF), jax.ShapeDtypeStruct((1024, TOK), BF), PIECE],
+        in_specs=[SM] * 2 + [VM] * 3 + [ANY] * 2,
+        out_specs=[VM] * 3,
+        scratch_shapes=BLOCK_SCRATCH,
         compiler_params=pltpu.CompilerParams(vmem_limit_bytes=40 * 1024 * 1024),
-        cost_estimate=pl.CostEstimate(flops=2 * TOK * 1024 * 8192, bytes_accessed=18 << 20, transcendentals=TOK * 512),
-        name="terms",
+        cost_estimate=pl.CostEstimate(flops=2 * TOK * 1024 * 2048, bytes_accessed=14 << 20, transcendentals=TOK * 512),
+        name="first_terms",
     )(tab, order, gate_pre, up_pre, hidden, wg, wu)
+
+
+def rest_terms(tab, order, gu, wg, wu):
+    return pl.pallas_call(
+        rest_kernel,
+        out_shape=[PIECE] * 3,
+        in_specs=[SM] * 2 + [VM] + [ANY] * 2,
+        out_specs=[VM] * 3,
+        scratch_shapes=BLOCK_SCRATCH,
+        compiler_params=pltpu.CompilerParams(vmem_limit_bytes=40 * 1024 * 1024),
+        cost_estimate=pl.CostEstimate(flops=2 * TOK * 1024 * 6144, bytes_accessed=16 << 20, transcendentals=0),
+        name="rest_terms",
+    )(tab, order, gu, wg, wu)
 
 
 def wgrad_kernel(
@@ -227,15 +241,8 @@
     return tab, order, lrow, lslot, lact, meta
 
 
-def gather_direct(value, axis):
-    return [value] + [shift(value, axis, k) for k in (1, 2, 3)]
-
-
-def gather_ring(value, axis):
-    parts = [value]
-    for _ in range(3):
-        parts.append(shift(parts[-1], axis, 1))
-    return parts
+def after(value, *others):
+    return lax.optimization_barrier((value, *others))[0]
 
 
 def body(
@@ -243,25 +250,42 @@
 ):
     tab, order, lrow, lslot, lact, meta = tables(block_rows, block_cols, block_count)
     both = jnp.stack([activations[:, :128], activations[:, 128:]])
-    near = gather_direct(both, "x")
-    even = jnp.stack([v[0] for v in near])
-    odd = jnp.stack([v[1] for v in near])
-    gut, t0, t1, t2, t3 = terms(tab, order, gate_pre, up_pre, hidden_grad, gate_blocks, up_blocks)
+    near = [both] + [shift(both, "x", k) for k in (1, 2, 3)]
+    gu, gut, t1 = first_terms(tab, order, gate_pre, up_pre, hidden_grad, gate_blocks, up_blocks)
+    moving = shift(t1, "x", 1)
     other = shift(gut, "yh", 1)
-    even = jnp.concatenate(gather_direct(even, "z"))
-    odd = jnp.concatenate(gather_direct(odd, "y"))
-    pieces = gather_ring(even, "y") + gather_ring(odd, "z")
-    moving = shift(t1, "x", 1)
-    moving = shift(add(moving, t2), "x", 1)
-    moving = shift(add(moving, t3), "x", 1)
+    even = after(jnp.stack([v[0] for v in near]), t1)
+    odd = after(jnp.stack([v[1] for v in near]), t1)
+    evens, odds = [even], [odd]
+    evens.append(shift(even, "z", 1))
+    odds.append(shift(odd, "y", 1))
+    t2, t3, t0 = rest_terms(tab, order, gu, gate_blocks, up_blocks)
+    evens.append(shift(after(evens[1], t2), "z", 1))
+    odds.append(shift(after(odds[1], t2), "y", 1))
+    evens.append(shift(evens[2], "z", 1))
+    odds.append(shift(odds[2], "y", 1))
+    moving = add(moving, t2)
+    evens = [after(jnp.concatenate(evens), moving, other)]
+    odds = [after(jnp.concatenate(odds), moving, other)]
+    moving = shift(moving, "x", 1)
+    evens.append(shift(evens[0], "y", 1))
+    odds.append(shift(odds[0], "z", 1))
+    moving = add(moving, t3)
+    evens.append(shift(after(evens[1], moving), "y", 1))
+    odds.append(shift(after(odds[1], moving), "z", 1))
+    moving = shift(moving, "x", 1)
     mine = add(moving, t0).reshape(4, 2, TOK, 256)
+    evens.append(shift(after(evens[2], mine), "y", 1))
+    odds.append(shift(after(odds[2], mine), "z", 1))
     moving = shift(mine[1], "z", 1)
-    moving = shift(add(moving, mine[2]), "z", 1)
+    moving = add(moving, mine[2])
+    meta = after(meta, moving)
+    moving = shift(moving, "z", 1)
     moving = shift(add(moving, mine[3]), "z", 1)
     keep = moving[0].astype(F32) + mine[0, 0].astype(F32)
     send = add(moving[1], mine[0, 1])
     input_grad = (keep + shift(send, "yl", 1).astype(F32)).astype(BF)
-    part = wgrad(lrow, lslot, lact, meta, gut, other, pieces)
+    part = wgrad(lrow, lslot, lact, meta, gut, other, evens + odds)
     total = add(part, shift(part, "c", 1))
     return input_grad, total[:, :128], total[:, 128:]
 

time: 264 us -> 212 us (0.80)
  waiting for transfers between devices: 165 us -> 114 us
  starting transfers between devices: 32.8 us -> 25.8 us
  other arithmetic: 7.5 us -> 12.6 us
    ppermute x21, waiting for transfers between devices: 160 us -> 108 us  [shift(): return lax.ppermute(value, AXES[axis], pairs)]
    ppermute x21, starting transfers between devices: 30.2 us -> 22.6 us  [shift(): return lax.ppermute(value, AXES[axis], pairs)]
    convert_element_type x7, other arithmetic: 5.26 us -> 9.28 us  [add(): return (a.astype(F32) + b.astype(F32)).astype(BF)]
    pallas_call x1 -> x2, Pallas kernels: 17.4 us -> 18.6 us  [the longest x1 11.7 us: rest_terms(): pl.pallas_call(rest_kernel, out_shape=[PIECE] * 3, in_specs=[SM] * 2 + [V...]
    unnamed x29 -> x30, local copies, waits for them, and re-layouts: 11.2 us -> 12.2 us
  transfers between devices with their start and end apart: 24 -> 24, of which waited for: 14 -> 11; matrix products, arithmetic and copies ran while one was open for 4% -> 5% of each run, Pallas kernels for 7% -> 9%
where the time goes in v2:
time: 212 us
  waiting for transfers between devices  114 us (54%)
  Pallas kernels  38.4 us (18%)
  starting transfers between devices  25.8 us (12%)
  local copies, waits for them, and re-layouts  19.7 us (9%)
  other arithmetic  12.6 us (6%)
    ppermute x21, waiting for transfers between devices, shift(): return lax.ppermute(value, AXES[axis], pairs)  108 us
    ppermute x21, starting transfers between devices, shift(): return lax.ppermute(value, AXES[axis], pairs)  22.6 us
    pallas_call x1, Pallas kernels, wgrad(): pl.pallas_call(wgrad_kernel, out_shape=jax.ShapeDtypeStruct((SLOTS, 256,...  19.8 us
    unnamed x30, local copies, waits for them, and re-layouts  12.2 us
    pallas_call x1, Pallas kernels, rest_terms(): pl.pallas_call(rest_kernel, out_shape=[PIECE] * 3, in_specs=[SM] * 2 + [V...  11.7 us
    convert_element_type x7, other arithmetic, add(): return (a.astype(F32) + b.astype(F32)).astype(BF)  9.28 us
    pallas_call x1, Pallas kernels, first_terms(): pl.pallas_call(first_kernel, out_shape=[jax.ShapeDtypeStruct((TOK, 1024),...  6.85 us
    ppermute x3, waiting for transfers between devices, shift(): return lax.ppermute(value, axis, [(0, 1), (1, 0)])  5.56 us
  transfers between devices with their start and end apart: 24, of which 11 were waited for; matrix products, arithmetic and copies ran while one was open for 5% of the time, Pallas kernels for 9%

profile of v2, /device:TPU:0, one launch (start us, length us, event | category | flops | bytes accessed | tf_op | source)
XLA Modules:
  0.0 211.8 jit_solution(8078965457932934328)
XLA Ops:
  1.6 2.9 %collective-permute-start.10 = (bf16[2,384,128]{2,1,0:T(8,128)(2,1)S(1)}, bf16[2,384,128]{2,1,0:T(8,128)(2,1)S(1)}, u32[]{:S(2)}, u32[]{:S(2)}) collective-permute-start(bf16[2,384,128]{2,1,0:T(8,128)(2,1)S(1)} %pad_maximum_fusion.4), channel_id=1, source_target_pairs={{0,24},{8,0},{16,8},{24,16},{32,40},{40,48},{48,56},{56,32},{1,25}... | collective-permute-start | bytes 589832 | tf_op jit(solution)/shard_map/ppermute | solution.py:36
  8.0 2.2 %copy-done = bf16[128,128,128]{2,1,0:T(8,128)(2,1)S(1)} copy-done((bf16[128,128,128]{2,1,0:T(8,128)(2,1)S(1)}, bf16[128,128,128]{2,1,0:T(8,128)(2,1)}, u32[]{:S(2)}) %copy-start) | copy-done | bytes 4194328
  10.1 2.2 %copy-done.2 = bf16[128,128,128]{2,1,0:T(8,128)(2,1)S(1)} copy-done((bf16[128,128,128]{2,1,0:T(8,128)(2,1)S(1)}, bf16[128,128,128]{2,1,0:T(8,128)(2,1)}, u32[]{:S(2)}) %copy-start.2) | copy-done | bytes 4194328
  15.3 6.9 %first_terms.1 = (bf16[384,1024]{1,0:T(8,128)(2,1)S(1)}, bf16[1024,384]{1,0:T(8,128)(2,1)}, bf16[8,384,256]{2,1,0:T(8,128)(2,1)S(1)}) custom-call(s32[256]{0:T(256)S(1)} %select_reduce_fusion.tab, s32[32]{0:T(128)S(1)} %mul.220.order, bf16[384,512]{1,0:T(8,128)(2,1)S(1)} %copy-done.4, bf16[384,512]{1,0:T(8,128)(2,1)S(1)} %copy-done.5, ...), custom_call_target="tpu_custom_call" | custom-call | flops 1610612736 | bytes 14680064 | tf_op jit(solution)/shard_map/first_terms/pallas_call | solution.py:101
  22.2 1.9 collective-permute-start
  24.3 2.0 collective-permute-start.11
  26.2 11.7 %rest_terms.1 = (bf16[8,384,256]{2,1,0:T(8,128)(2,1)S(1)}, bf16[8,384,256]{2,1,0:T(8,128)(2,1)S(1)}, bf16[8,384,256]{2,1,0:T(8,128)(2,1)S(1)}) custom-call(s32[256]{0:T(256)S(1)} %select_reduce_fusion.tab, s32[32]{0:T(128)S(1)} %mul.220.order, bf16[384,1024]{1,0:T(8,128)(2,1)S(1)} %get-tuple-element.21.gu, bf16[128,128,128]{2,1,0:T(8,128)(2,1)S(1)} %copy-done.1, ...), custom_call_target="tpu_custom_call" | custom-call | flops 4831838208 | bytes 16777216 | tf_op jit(solution)/shard_map/rest_terms/pallas_call | solution.py:114
  39.6 1.9 collective-permute-start.12
  41.6 2.9 %collective-permute-start.7 = (bf16[1024,384]{1,0:T(8,128)(2,1)}, bf16[1024,384]{1,0:T(8,128)(2,1)S(1)}, u32[]{:S(2)}, u32[]{:S(2)}) collective-permute-start(bf16[1024,384]{1,0:T(8,128)(2,1)} %get-tuple-element.26.own_ref), channel_id=1, source_target_pairs={{0,64},{64,0},{1,65},{65,1},{2,66},{66,2},{3,67},{67,3},{4,68},{68... | collective-permute-start | bytes 2359304 | tf_op jit(solution)/shard_map/ppermute | solution.py:24
  44.5 4.1 %collective-permute-done.17 = bf16[4,384,128]{2,1,0:T(8,128)(2,1)S(1)} collective-permute-done((bf16[4,384,128]{2,1,0:T(8,128)(2,1)S(1)}, bf16[4,384,128]{2,1,0:T(8,128)(2,1)S(1)}, u32[]{:S(2)}, u32[]{:S(2)}) %collective-permute-start.17) | collective-permute-done | bytes 393248 | tf_op jit(solution)/shard_map/ppermute | solution.py:36
  50.1 2.3 %collective-permute-start.13 = (bf16[4,384,128]{2,1,0:T(8,128)(2,1)S(1)}, bf16[4,384,128]{2,1,0:T(8,128)(2,1)S(1)}, u32[]{:S(2)}, u32[]{:S(2)}) collective-permute-start(bf16[4,384,128]{2,1,0:T(8,128)(2,1)S(1)} %collective-permute-done.12), channel_id=1, source_target_pairs={{0,2},{2,4},{4,6},{6,0},{32,38},{34,32},{36,34},{38,36},{1,3},{3,5... | collective-permute-start | bytes 1179656 | tf_op jit(solution)/shard_map/ppermute | solution.py:36
  52.9 16.5 %collective-permute-done.18 = bf16[4,384,128]{2,1,0:T(8,128)(2,1)S(1)} collective-permute-done((bf16[4,384,128]{2,1,0:T(8,128)(2,1)S(1)}, bf16[4,384,128]{2,1,0:T(8,128)(2,1)S(1)}, u32[]{:S(2)}, u32[]{:S(2)}) %collective-permute-start.18) | collective-permute-done | bytes 393248 | tf_op jit(solution)/shard_map/ppermute | solution.py:36
  71.3 7.0 %collective-permute-done.19 = bf16[4,384,128]{2,1,0:T(8,128)(2,1)S(1)} collective-permute-done((bf16[4,384,128]{2,1,0:T(8,128)(2,1)S(1)}, bf16[4,384,128]{2,1,0:T(8,128)(2,1)S(1)}, u32[]{:S(2)}, u32[]{:S(2)}) %collective-permute-start.19) | collective-permute-done | bytes 393248 | tf_op jit(solution)/shard_map/ppermute | solution.py:36
  79.4 1.9 collective-permute-start.20
  82.4 18.6 %collective-permute-done.20.rest_5_ = bf16[16,384,128]{2,1,0:T(8,128)(2,1)S(1)} collective-permute-done((bf16[16,384,128]{2,1,0:T(8,128)(2,1)S(1)}, bf16[16,384,128]{2,1,0:T(8,128)(2,1)S(1)}, u32[]{:S(2)}, u32[]{:S(2)}) %collective-permute-start.20) | collective-permute-done | bytes 1572896 | tf_op jit(solution)/shard_map/ppermute | solution.py:36
  101.1 1.9 collective-permute-done.14.rest_1_
  105.6 19.1 %collective-permute-done.21.rest_6_ = bf16[16,384,128]{2,1,0:T(8,128)(2,1)} collective-permute-done((bf16[16,384,128]{2,1,0:T(8,128)(2,1)S(1)}, bf16[16,384,128]{2,1,0:T(8,128)(2,1)}, u32[]{:S(2)}, u32[]{:S(2)}) %collective-permute-start.21) | collective-permute-done | bytes 1572896 | tf_op jit(solution)/shard_map/ppermute | solution.py:36
  130.0 22.7 %collective-permute-done.3 = bf16[2,384,256]{2,1,0:T(8,128)(2,1)} collective-permute-done((bf16[2,384,256]{2,1,0:T(8,128)(2,1)S(1)}, bf16[2,384,256]{2,1,0:T(8,128)(2,1)}, u32[]{:S(2)}, u32[]{:S(2)}) %collective-permute-start.3) | collective-permute-done | bytes 393248 | tf_op jit(solution)/shard_map/ppermute | solution.py:36
  157.9 19.8 %wgrad.1 = bf16[128,256,128]{2,1,0:T(8,128)(2,1)} custom-call(s32[144]{0:T(256)S(1)} %get-tuple-element.39.lrow, s32[144]{0:T(256)S(1)} %get-tuple-element.38.lslot, s32[288]{0:T(512)S(1)} %reshape.594.lact, s32[3]{0:T(128)S(1)} %pad_add_fusion.1.meta, bf16[1024,384]{1,0:T(8,128)(2,1)} %get-tuple-element.26.own_ref, bf16[1024,384]{1,0:T(8,128)(2,1)S(1)} %copy-done.12, ...), custom_call_target="tpu_custom_call" | custom-call | flops 6442450944 | bytes 23068672 | tf_op jit(solution)/shard_map/wgrad/pallas_call | solution.py:171
  177.9 9.0 %collective-permute-done.4 = bf16[2,384,256]{2,1,0:T(8,128)(2,1)S(1)} collective-permute-done((bf16[2,384,256]{2,1,0:T(8,128)(2,1)S(1)}, bf16[2,384,256]{2,1,0:T(8,128)(2,1)S(1)}, u32[]{:S(2)}, u32[]{:S(2)}) %collective-permute-start.4) | collective-permute-done | bytes 393248 | tf_op jit(solution)/shard_map/ppermute | solution.py:36
  187.0 9.0 %collective-permute-done.5 = bf16[2,384,256]{2,1,0:T(8,128)(2,1)S(1)} collective-permute-done((bf16[2,384,256]{2,1,0:T(8,128)(2,1)S(1)}, bf16[2,384,256]{2,1,0:T(8,128)(2,1)S(1)}, u32[]{:S(2)}, u32[]{:S(2)}) %collective-permute-start.5) | collective-permute-done | bytes 393248 | tf_op jit(solution)/shard_map/ppermute | solution.py:36
  196.2 5.6 %collective-permute-done.6 = bf16[384,256]{1,0:T(8,128)(2,1)S(1)} collective-permute-done((bf16[384,256]{1,0:T(8,128)(2,1)S(1)}, bf16[384,256]{1,0:T(8,128)(2,1)S(1)}, u32[]{:S(2)}, u32[]{:S(2)}) %collective-permute-start.6) | collective-permute-done | bytes 196640 | tf_op jit(solution)/shard_map/ppermute | solution.py:24
  202.6 5.6 %add_convert_fusion = bf16[128,256,128]{2,1,0:T(8,128)(2,1)S(1)} fusion(bf16[128,256,128]{2,1,0:T(8,128)(2,1)S(1)} %collective-permute-done.23, bf16[128,256,128]{2,1,0:T(8,128)(2,1)} %wgrad.1), kind=kLoop, calls=%fused_computation | loop fusion | flops 16777216 | bytes 25165824 | tf_op jit(solution)/shard_map/convert_element_type | solution.py:40
  208.2 3.7 %fusion.13 = (bf16[128,128,128]{2,1,0:T(8,128)(2,1)}, bf16[128,128,128]{2,1,0:T(8,128)(2,1)}) fusion(bf16[128,256,128]{2,1,0:T(8,128)(2,1)S(1)} %add_convert_fusion), kind=kLoop, calls=%fused_computation.95 | loop fusion | bytes 16777216 | tf_op jit(solution)/shard_map/slice | solution.py:290
  (103 shorter events, 29.0 us)
Async XLA Ops:
  1.6 22.4 %collective-permute-start.10 = (bf16[2,384,128]{2,1,0:T(8,128)(2,1)S(1)}, bf16[2,384,128]{2,1,0:T(8,128)(2,1)S(1)}, u32[]{:S(2)}, u32[]{:S(2)}) collective-permute-start(bf16[2,384,128]{2,1,0:T(8,128)(2,1)S(1)} %pad_maximum_fusion.4), channel_id=1, source_target_pairs={{0,24},{8,0},{16,8},{24,16},{32,40},{40,48},{48,56},{56,32},{1,25}... | collective-permute-start | bytes 589832 | tf_op jit(solution)/shard_map/ppermute | solution.py:36
  4.5 19.6 %collective-permute-start.9 = (bf16[2,384,128]{2,1,0:T(8,128)(2,1)S(1)}, bf16[2,384,128]{2,1,0:T(8,128)(2,1)S(1)}, u32[]{:S(2)}, u32[]{:S(2)}) collective-permute-start(bf16[2,384,128]{2,1,0:T(8,128)(2,1)S(1)} %pad_maximum_fusion.4), channel_id=1, source_target_pairs={{0,16},{8,24},{16,0},{24,8},{32,48},{40,56},{48,32},{56,40},{1,17}... | collective-permute-start | bytes 589832 | tf_op jit(solution)/shard_map/ppermute | solution.py:36
  5.3 18.8 %collective-permute-start.8 = (bf16[2,384,128]{2,1,0:T(8,128)(2,1)S(1)}, bf16[2,384,128]{2,1,0:T(8,128)(2,1)S(1)}, u32[]{:S(2)}, u32[]{:S(2)}) collective-permute-start(bf16[2,384,128]{2,1,0:T(8,128)(2,1)S(1)} %pad_maximum_fusion.4), channel_id=1, source_target_pairs={{0,8},{8,16},{16,24},{24,0},{32,56},{40,32},{48,40},{56,48},{1,9},... | collective-permute-start | bytes 589832 | tf_op jit(solution)/shard_map/ppermute | solution.py:36
  22.2 30.2 %collective-permute-start = (bf16[8,384,256]{2,1,0:T(8,128)(2,1)S(1)}, bf16[8,384,256]{2,1,0:T(8,128)(2,1)S(1)}, u32[]{:S(2)}, u32[]{:S(2)}) collective-permute-start(bf16[8,384,256]{2,1,0:T(8,128)(2,1)S(1)} %get-tuple-element.20), channel_id=1, source_target_pairs={{0,8},{8,16},{16,24},{24,0},{32,56},{40,32},{48,40},{56,48},{1,9},... | collective-permute-start | bytes 4718600 | tf_op jit(solution)/shard_map/ppermute | solution.py:36
  24.3 15.4 %collective-permute-start.11 = (bf16[4,384,128]{2,1,0:T(8,128)(2,1)S(1)}, bf16[4,384,128]{2,1,0:T(8,128)(2,1)S(1)}, u32[]{:S(2)}, u32[]{:S(2)}) collective-permute-start(bf16[4,384,128]{2,1,0:T(8,128)(2,1)S(1)} %get-tuple-element.27), channel_id=1, source_target_pairs={{0,2},{2,4},{4,6},{6,0},{32,38},{34,32},{36,34},{38,36},{1,3},{3,5... | collective-permute-start | bytes 1179656 | tf_op jit(solution)/shard_map/ppermute | solution.py:36
  38.0 10.5 %collective-permute-start.17 = (bf16[4,384,128]{2,1,0:T(8,128)(2,1)S(1)}, bf16[4,384,128]{2,1,0:T(8,128)(2,1)S(1)}, u32[]{:S(2)}, u32[]{:S(2)}) collective-permute-start(bf16[4,384,128]{2,1,0:T(8,128)(2,1)S(1)} %get-tuple-element.32), channel_id=1, source_target_pairs={{0,1},{1,64},{32,97},{33,32},{64,65},{65,0},{96,33},{97,96},{2,3},... | collective-permute-start | bytes 1179656 | tf_op jit(solution)/shard_map/ppermute | solution.py:36
  39.6 10.5 %collective-permute-start.12 = (bf16[4,384,128]{2,1,0:T(8,128)(2,1)S(1)}, bf16[4,384,128]{2,1,0:T(8,128)(2,1)S(1)}, u32[]{:S(2)}, u32[]{:S(2)}) collective-permute-start(bf16[4,384,128]{2,1,0:T(8,128)(2,1)S(1)} %collective-permute-done.11), channel_id=1, source_target_pairs={{0,2},{2,4},{4,6},{6,0},{32,38},{34,32},{36,34},{38,36},{1,3},{3,5... | collective-permute-start | bytes 1179656 | tf_op jit(solution)/shard_map/ppermute | solution.py:36
  41.6 37.0 %collective-permute-start.7 = (bf16[1024,384]{1,0:T(8,128)(2,1)}, bf16[1024,384]{1,0:T(8,128)(2,1)S(1)}, u32[]{:S(2)}, u32[]{:S(2)}) collective-permute-start(bf16[1024,384]{1,0:T(8,128)(2,1)} %get-tuple-element.26.own_ref), channel_id=1, source_target_pairs={{0,64},{64,0},{1,65},{65,1},{2,66},{66,2},{3,67},{67,3},{4,68},{68... | collective-permute-start | bytes 2359304 | tf_op jit(solution)/shard_map/ppermute | solution.py:24
  48.5 20.8 %collective-permute-start.18 = (bf16[4,384,128]{2,1,0:T(8,128)(2,1)S(1)}, bf16[4,384,128]{2,1,0:T(8,128)(2,1)S(1)}, u32[]{:S(2)}, u32[]{:S(2)}) collective-permute-start(bf16[4,384,128]{2,1,0:T(8,128)(2,1)S(1)} %collective-permute-done.17), channel_id=1, source_target_pairs={{0,1},{1,64},{32,97},{33,32},{64,65},{65,0},{96,33},{97,96},{2,3},... | collective-permute-start | bytes 1179656 | tf_op jit(solution)/shard_map/ppermute | solution.py:36
  50.1 21.0 %collective-permute-start.13 = (bf16[4,384,128]{2,1,0:T(8,128)(2,1)S(1)}, bf16[4,384,128]{2,1,0:T(8,128)(2,1)S(1)}, u32[]{:S(2)}, u32[]{:S(2)}) collective-permute-start(bf16[4,384,128]{2,1,0:T(8,128)(2,1)S(1)} %collective-permute-done.12), channel_id=1, source_target_pairs={{0,2},{2,4},{4,6},{6,0},{32,38},{34,32},{36,34},{38,36},{1,3},{3,5... | collective-permute-start | bytes 1179656 | tf_op jit(solution)/shard_map/ppermute | solution.py:36
  52.8 29.2 %collective-permute-start.1 = (bf16[8,384,256]{2,1,0:T(8,128)(2,1)S(1)}, bf16[8,384,256]{2,1,0:T(8,128)(2,1)S(1)}, u32[]{:S(2)}, u32[]{:S(2)}) collective-permute-start(bf16[8,384,256]{2,1,0:T(8,128)(2,1)S(1)} %add_convert_fusion.3), channel_id=1, source_target_pairs={{0,8},{8,16},{16,24},{24,0},{32,56},{40,32},{48,40},{56,48},{1,9},... | collective-permute-start | bytes 4718600 | tf_op jit(solution)/shard_map/ppermute | solution.py:36
  69.4 9.0 %collective-permute-start.19 = (bf16[4,384,128]{2,1,0:T(8,128)(2,1)S(1)}, bf16[4,384,128]{2,1,0:T(8,128)(2,1)S(1)}, u32[]{:S(2)}, u32[]{:S(2)}) collective-permute-start(bf16[4,384,128]{2,1,0:T(8,128)(2,1)S(1)} %collective-permute-done.18), channel_id=1, source_target_pairs={{0,1},{1,64},{32,97},{33,32},{64,65},{65,0},{96,33},{97,96},{2,3},... | collective-permute-start | bytes 1179656 | tf_op jit(solution)/shard_map/ppermute | solution.py:36
  79.4 21.6 %collective-permute-start.20 = (bf16[16,384,128]{2,1,0:T(8,128)(2,1)S(1)}, bf16[16,384,128]{2,1,0:T(8,128)(2,1)S(1)}, u32[]{:S(2)}, u32[]{:S(2)}) collective-permute-start(bf16[16,384,128]{2,1,0:T(8,128)(2,1)S(1)} %pad_maximum_fusion.1.rest_4_), channel_id=1, source_target_pairs={{0,2},{2,4},{4,6},{6,0},{32,38},{34,32},{36,34},{38,36},{1,3},{3,5... | collective-permute-start | bytes 4718600 | tf_op jit(solution)/shard_map/ppermute | solution.py:36
  81.4 21.6 %collective-permute-start.14 = (bf16[16,384,128]{2,1,0:T(8,128)(2,1)S(1)}, bf16[16,384,128]{2,1,0:T(8,128)(2,1)S(1)}, u32[]{:S(2)}, u32[]{:S(2)}) collective-permute-start(bf16[16,384,128]{2,1,0:T(8,128)(2,1)S(1)} %pad_maximum_fusion.rest_0_), channel_id=1, source_target_pairs={{0,1},{1,64},{32,97},{33,32},{64,65},{65,0},{96,33},{97,96},{2,3},... | collective-permute-start | bytes 4718600 | tf_op jit(solution)/shard_map/ppermute | solution.py:36
  82.3 21.7 %collective-permute-start.2 = (bf16[8,384,256]{2,1,0:T(8,128)(2,1)S(1)}, bf16[8,384,256]{2,1,0:T(8,128)(2,1)S(1)}, u32[]{:S(2)}, u32[]{:S(2)}) collective-permute-start(bf16[8,384,256]{2,1,0:T(8,128)(2,1)S(1)} %add_convert_fusion.2), channel_id=1, source_target_pairs={{0,8},{8,16},{16,24},{24,0},{32,56},{40,32},{48,40},{56,48},{1,9},... | collective-permute-start | bytes 4718600 | tf_op jit(solution)/shard_map/ppermute | solution.py:36
  103.0 21.7 %collective-permute-start.15 = (bf16[16,384,128]{2,1,0:T(8,128)(2,1)S(1)}, bf16[16,384,128]{2,1,0:T(8,128)(2,1)}, u32[]{:S(2)}, u32[]{:S(2)}) collective-permute-start(bf16[16,384,128]{2,1,0:T(8,128)(2,1)S(1)} %collective-permute-done.14.rest_1_), channel_id=1, source_target_pairs={{0,1},{1,64},{32,97},{33,32},{64,65},{65,0},{96,33},{97,96},{2,3},... | collective-permute-start | bytes 4718600 | tf_op jit(solution)/shard_map/ppermute | solution.py:36
  103.0 21.7 %collective-permute-start.21 = (bf16[16,384,128]{2,1,0:T(8,128)(2,1)S(1)}, bf16[16,384,128]{2,1,0:T(8,128)(2,1)}, u32[]{:S(2)}, u32[]{:S(2)}) collective-permute-start(bf16[16,384,128]{2,1,0:T(8,128)(2,1)S(1)} %collective-permute-done.20.rest_5_), channel_id=1, source_target_pairs={{0,2},{2,4},{4,6},{6,0},{32,38},{34,32},{36,34},{38,36},{1,3},{3,5... | collective-permute-start | bytes 4718600 | tf_op jit(solution)/shard_map/ppermute | solution.py:36
  124.7 29.2 %collective-permute-start.16 = (bf16[16,384,128]{2,1,0:T(8,128)(2,1)}, bf16[16,384,128]{2,1,0:T(8,128)(2,1)}, u32[]{:S(2)}, u32[]{:S(2)}) collective-permute-start(bf16[16,384,128]{2,1,0:T(8,128)(2,1)} %collective-permute-done.15.rest_2_), channel_id=1, source_target_pairs={{0,1},{1,64},{32,97},{33,32},{64,65},{65,0},{96,33},{97,96},{2,3},... | collective-permute-start | bytes 4718600 | tf_op jit(solution)/shard_map/ppermute | solution.py:36
  126.6 27.4 %collective-permute-start.22 = (bf16[16,384,128]{2,1,0:T(8,128)(2,1)}, bf16[16,384,128]{2,1,0:T(8,128)(2,1)}, u32[]{:S(2)}, u32[]{:S(2)}) collective-permute-start(bf16[16,384,128]{2,1,0:T(8,128)(2,1)} %collective-permute-done.21.rest_6_), channel_id=1, source_target_pairs={{0,2},{2,4},{4,6},{6,0},{32,38},{34,32},{36,34},{38,36},{1,3},{3,5... | collective-permute-start | bytes 4718600 | tf_op jit(solution)/shard_map/ppermute | solution.py:36
  127.9 24.9 %collective-permute-start.3 = (bf16[2,384,256]{2,1,0:T(8,128)(2,1)S(1)}, bf16[2,384,256]{2,1,0:T(8,128)(2,1)}, u32[]{:S(2)}, u32[]{:S(2)}) collective-permute-start(bf16[2,384,256]{2,1,0:T(8,128)(2,1)S(1)} %slice.71), channel_id=1, source_target_pairs={{0,2},{2,4},{4,6},{6,0},{32,38},{34,32},{36,34},{38,36},{1,3},{3,5... | collective-permute-start | bytes 1179656 | tf_op jit(solution)/shard_map/ppermute | solution.py:36
  177.7 24.9 %collective-permute-start.23 = (bf16[128,256,128]{2,1,0:T(8,128)(2,1)}, bf16[128,256,128]{2,1,0:T(8,128)(2,1)S(1)}, u32[]{:S(2)}, u32[]{:S(2)}) collective-permute-start(bf16[128,256,128]{2,1,0:T(8,128)(2,1)} %wgrad.1), channel_id=1, source_target_pairs={{0,32},{32,0},{1,33},{33,1},{2,34},{34,2},{3,35},{35,3},{4,36},{36... | collective-permute-start | bytes 25165832 | tf_op jit(solution)/shard_map/ppermute | solution.py:24
  177.8 9.1 %collective-permute-start.4 = (bf16[2,384,256]{2,1,0:T(8,128)(2,1)S(1)}, bf16[2,384,256]{2,1,0:T(8,128)(2,1)S(1)}, u32[]{:S(2)}, u32[]{:S(2)}) collective-permute-start(bf16[2,384,256]{2,1,0:T(8,128)(2,1)S(1)} %add_convert_fusion.5), channel_id=1, source_target_pairs={{0,2},{2,4},{4,6},{6,0},{32,38},{34,32},{36,34},{38,36},{1,3},{3,5... | collective-permute-start | bytes 1179656 | tf_op jit(solution)/shard_map/ppermute | solution.py:36
  186.9 9.1 %collective-permute-start.5 = (bf16[2,384,256]{2,1,0:T(8,128)(2,1)S(1)}, bf16[2,384,256]{2,1,0:T(8,128)(2,1)S(1)}, u32[]{:S(2)}, u32[]{:S(2)}) collective-permute-start(bf16[2,384,256]{2,1,0:T(8,128)(2,1)S(1)} %add_convert_fusion.4), channel_id=1, source_target_pairs={{0,2},{2,4},{4,6},{6,0},{32,38},{34,32},{36,34},{38,36},{1,3},{3,5... | collective-permute-start | bytes 1179656 | tf_op jit(solution)/shard_map/ppermute | solution.py:36
  196.1 5.7 %collective-permute-start.6 = (bf16[384,256]{1,0:T(8,128)(2,1)S(1)}, bf16[384,256]{1,0:T(8,128)(2,1)S(1)}, u32[]{:S(2)}, u32[]{:S(2)}) collective-permute-start(bf16[384,256]{1,0:T(8,128)(2,1)S(1)} %fusion), channel_id=1, source_target_pairs={{0,1},{1,0},{2,3},{3,2},{4,5},{5,4},{6,7},{7,6},{8,9},{9,8},{10,11... | collective-permute-start | bytes 589832 | tf_op jit(solution)/shard_map/ppermute | solution.py:24
  (15 other events, 92.7 us)

commit v3 on v2

--- a/solution.py
+++ b/solution.py
@@ -40,86 +40,64 @@
     return (a.astype(F32) + b.astype(F32)).astype(BF)
 
 
-def load_blocks(wg_hbm, wu_hbm, wbuf, wsem):
-    copies = [
-        pltpu.make_async_copy(wg_hbm, wbuf.at[pl.ds(0, SLOTS), pl.ds(0, 128), :], wsem.at[0]),
-        pltpu.make_async_copy(wu_hbm, wbuf.at[pl.ds(0, SLOTS), pl.ds(128, 128), :], wsem.at[1]),
-    ]
-    for copy in copies:
-        copy.start()
-    wbuf[SLOTS] = jnp.zeros((256, 128), BF)
-    return copies
-
-
-def term_chunk(k, tab, order, gu, wbuf, out):
+def gates_kernel(gate_ref, up_ref, hid_ref, gu, gut):
+    g = gate_ref[...].astype(F32)
+    u = up_ref[...].astype(F32)
+    h = hid_ref[...].astype(F32)
+    sig = 1.0 / (1.0 + jnp.exp(-g))
+    gg = h * u * sig * (1.0 + g * (1.0 - sig))
+    ug = h * g * sig
+    gu[:, :128] = gg.astype(BF)
+    gu[:, 128:] = ug.astype(BF)
+    gut[:128, :] = gg.T.astype(BF)
+    gut[128:, :] = ug.T.astype(BF)
+
+
+def chunk_kernel(k, tab, order, gu, wg, wu, out):
     @pl.loop(0, 8)
     def _(j):
         base = order[k * 8 + j]
         total = jnp.zeros((TOK, 256), F32)
         for r in range(4):
-            left = wbuf[tab[r * 64 + base]]
-            right = wbuf[tab[r * 64 + base + 1]]
-            both = jnp.concatenate([left, right], axis=1)
+            sides = []
+            for side in range(2):
+                slot = tab[r * 64 + base + side]
+                index = jnp.minimum(slot, SLOTS - 1)
+                block = jnp.concatenate([wg[index], wu[index]], axis=0)
+                sides.append(jnp.where(slot < SLOTS, block, jnp.zeros_like(block)))
+            both = jnp.concatenate(sides, axis=1)
             total += jnp.dot(gu[:, r * 256 : (r + 1) * 256], both, preferred_element_type=F32)
         out[j] = total.astype(BF)
-
-
-def first_kernel(tab, order, gate_ref, up_ref, hid_ref, wg_hbm, wu_hbm, gu, gut_ref, t1, wbuf, wsem):
-    copies = load_blocks(wg_hbm, wu_hbm, wbuf, wsem)
-    for r in range(4):
-        cols = pl.ds(r * 128, 128)
-        g = gate_ref[:, cols].astype(F32)
-        u = up_ref[:, cols].astype(F32)
-        h = hid_ref[:, cols].astype(F32)
-        sig = 1.0 / (1.0 + jnp.exp(-g))
-        gg = h * u * sig * (1.0 + g * (1.0 - sig))
-        ug = h * g * sig
-        gu[:, pl.ds(r * 256, 128)] = gg.astype(BF)
-        gu[:, pl.ds(r * 256 + 128, 128)] = ug.astype(BF)
-        gut_ref[pl.ds(r * 256, 128), :] = gg.T.astype(BF)
-        gut_ref[pl.ds(r * 256 + 128, 128), :] = ug.T.astype(BF)
-    for copy in copies:
-        copy.wait()
-    term_chunk(1, tab, order, gu, wbuf, t1)
-
-
-def rest_kernel(tab, order, gu, wg_hbm, wu_hbm, t2, t3, t0, wbuf, wsem):
-    for copy in load_blocks(wg_hbm, wu_hbm, wbuf, wsem):
-        copy.wait()
-    for k, out in ((2, t2), (3, t3), (0, t0)):
-        term_chunk(k, tab, order, gu, wbuf, out)
 
 
 PIECE = jax.ShapeDtypeStruct((8, TOK, 256), BF)
 VM = pl.BlockSpec(memory_space=pltpu.VMEM)
 SM = pl.BlockSpec(memory_space=pltpu.SMEM)
 ANY = pl.BlockSpec(memory_space=pl.ANY)
-BLOCK_SCRATCH = [pltpu.VMEM((SLOTS + 1, 256, 128), BF), pltpu.SemaphoreType.DMA((2,))]
-
-
-def first_terms(tab, order, gate_pre, up_pre, hidden, wg, wu):
+
+
+def gates(gate_pre, up_pre, hidden):
     return pl.pallas_call(
-        first_kernel,
-        out_shape=[jax.ShapeDtypeStruct((TOK, 1024), BF), jax.ShapeDtypeStruct((1024, TOK), BF), PIECE],
-        in_specs=[SM] * 2 + [VM] * 3 + [ANY] * 2,
-        out_specs=[VM] * 3,
-        scratch_shapes=BLOCK_SCRATCH,
-        compiler_params=pltpu.CompilerParams(vmem_limit_bytes=40 * 1024 * 1024),
-        cost_estimate=pl.CostEstimate(flops=2 * TOK * 1024 * 2048, bytes_accessed=14 << 20, transcendentals=TOK * 512),
-        name="first_terms",
-    )(tab, order, gate_pre, up_pre, hidden, wg, wu)
-
-
-def rest_terms(tab, order, gu, wg, wu):
+        gates_kernel,
+        out_shape=[jax.ShapeDtypeStruct((TOK, 1024), BF), jax.ShapeDtypeStruct((1024, TOK), BF)],
+        grid=(4,),
+        in_specs=[pl.BlockSpec((TOK, 128), lambda r: (0, r))] * 3,
+        out_specs=[pl.BlockSpec((TOK, 256), lambda r: (0, r)), pl.BlockSpec((256, TOK), lambda r: (r, 0))],
+        compiler_params=pltpu.CompilerParams(vmem_limit_bytes=16 * 1024 * 1024),
+        cost_estimate=pl.CostEstimate(flops=TOK * 512 * 20, bytes_accessed=3 << 20, transcendentals=TOK * 512),
+        name="gates",
+    )(gate_pre, up_pre, hidden)
+
+
+def terms(k, tab, order, gu, wg, wu):
     return pl.pallas_call(
-        rest_kernel,
-        out_shape=[PIECE] * 3,
-        in_specs=[SM] * 2 + [VM] + [ANY] * 2,
-        out_specs=[VM] * 3,
-        scratch_shapes=BLOCK_SCRATCH,
-        compiler_params=pltpu.CompilerParams(vmem_limit_bytes=40 * 1024 * 1024),
-        cost_estimate=pl.CostEstimate(flops=2 * TOK * 1024 * 6144, bytes_accessed=16 << 20, transcendentals=0),
-        name="rest_terms",
+        functools.partial(chunk_kernel, k),
+        out_shape=PIECE,
+        in_specs=[SM] * 2 + [VM] * 3,
+        out_specs=VM,
+        compiler_params=pltpu.CompilerParams(vmem_limit_bytes=24 * 1024 * 1024),
+        cost_estimate=pl.CostEstimate(flops=2 * TOK * 1024 * 2048, bytes_accessed=10 << 20, transcendentals=0),
+        name="terms",
     )(tab, order, gu, wg, wu)
 
 
@@ -166,13 +144,11 @@
 
 
 def wgrad(lrow, lslot, lact, meta, own, other, pieces):
-    vm = pl.BlockSpec(memory_space=pltpu.VMEM)
-    anyspace = pl.BlockSpec(memory_space=pl.ANY)
     return pl.pallas_call(
         wgrad_kernel,
         out_shape=jax.ShapeDtypeStruct((SLOTS, 256, 128), BF),
-        in_specs=[pl.BlockSpec(memory_space=pltpu.SMEM)] * 4 + [vm] * 2 + [anyspace] * 8,
-        out_specs=anyspace,
+        in_specs=[SM] * 4 + [VM] * 2 + [ANY] * 8,
+        out_specs=ANY,
         scratch_shapes=[
             pltpu.VMEM((128, TOK, 128), BF),
             pltpu.VMEM((1024, 2 * TOK), BF),
@@ -251,22 +227,25 @@
     tab, order, lrow, lslot, lact, meta = tables(block_rows, block_cols, block_count)
     both = jnp.stack([activations[:, :128], activations[:, 128:]])
     near = [both] + [shift(both, "x", k) for k in (1, 2, 3)]
-    gu, gut, t1 = first_terms(tab, order, gate_pre, up_pre, hidden_grad, gate_blocks, up_blocks)
+    gu, gut = gates(gate_pre, up_pre, hidden_grad)
+    other = shift(gut, "yh", 1)
+    t1 = terms(1, tab, order, gu, gate_blocks, up_blocks)
     moving = shift(t1, "x", 1)
-    other = shift(gut, "yh", 1)
     even = after(jnp.stack([v[0] for v in near]), t1)
     odd = after(jnp.stack([v[1] for v in near]), t1)
     evens, odds = [even], [odd]
     evens.append(shift(even, "z", 1))
     odds.append(shift(odd, "y", 1))
-    t2, t3, t0 = rest_terms(tab, order, gu, gate_blocks, up_blocks)
+    t2 = terms(2, tab, order, after(gu, even, odd), gate_blocks, up_blocks)
     evens.append(shift(after(evens[1], t2), "z", 1))
     odds.append(shift(after(odds[1], t2), "y", 1))
-    evens.append(shift(evens[2], "z", 1))
-    odds.append(shift(odds[2], "y", 1))
+    t3 = terms(3, tab, order, after(gu, evens[1], odds[1]), gate_blocks, up_blocks)
+    evens.append(shift(after(evens[2], t3, other), "z", 1))
+    odds.append(shift(after(odds[2], t3, other), "y", 1))
+    t0 = terms(0, tab, order, after(gu, evens[2], odds[2]), gate_blocks, up_blocks)
     moving = add(moving, t2)
-    evens = [after(jnp.concatenate(evens), moving, other)]
-    odds = [after(jnp.concatenate(odds), moving, other)]
+    evens = [after(jnp.concatenate(evens), t0, moving)]
+    odds = [after(jnp.concatenate(odds), t0, moving)]
     moving = shift(moving, "x", 1)
     evens.append(shift(evens[0], "y", 1))
     odds.append(shift(odds[0], "z", 1))

time: 212 us -> 199 us (0.939); the launches traced: 212 us -> 197 us
  Pallas kernels: 38.4 us -> 30 us
  waiting for transfers between devices: 114 us -> 106 us
    ppermute x21, waiting for transfers between devices: 108 us -> 102 us  [shift(): return lax.ppermute(value, AXES[axis], pairs)]
    pallas_call x1, Pallas kernels: 19.8 us -> 14.5 us  [wgrad(): pl.pallas_call(wgrad_kernel, out_shape=jax.ShapeDtypeStruct((SLOTS, 256,...]
    pallas_call x2 -> x5, Pallas kernels: 18.6 us -> 15.5 us  [the longest x4 14.4 us: terms(): pl.pallas_call(functools.partial(chunk_kernel, k), out_shape=PIECE, in_sp...]
  transfers between devices with their start and end apart: 24 -> 24, of which waited for: 11 -> 14; matrix products, arithmetic and copies ran while one was open for 5% -> 5% of each run, Pallas kernels for 9% -> 8%
where the time goes in v3:
time: 199 us; the launch traced here: 197 us
  waiting for transfers between devices  106 us (53%)
  Pallas kernels  30 us (15%)
  starting transfers between devices  25.2 us (13%)
  local copies, waits for them, and re-layouts  20.7 us (10%)
  other arithmetic  12.6 us (6%)
    ppermute x21, waiting for transfers between devices, shift(): return lax.ppermute(value, AXES[axis], pairs)  102 us
    ppermute x21, starting transfers between devices, shift(): return lax.ppermute(value, AXES[axis], pairs)  20.6 us
    pallas_call x1, Pallas kernels, wgrad(): pl.pallas_call(wgrad_kernel, out_shape=jax.ShapeDtypeStruct((SLOTS, 256,...  14.5 us
    pallas_call x4, Pallas kernels, terms(): pl.pallas_call(functools.partial(chunk_kernel, k), out_shape=PIECE, in_sp...  14.4 us
    unnamed x30, local copies, waits for them, and re-layouts  13.1 us
    convert_element_type x7, other arithmetic, add(): return (a.astype(F32) + b.astype(F32)).astype(BF)  9.28 us
    ppermute x3, starting transfers between devices, shift(): return lax.ppermute(value, axis, [(0, 1), (1, 0)])  4.6 us
    ppermute x3, waiting for transfers between devices, shift(): return lax.ppermute(value, axis, [(0, 1), (1, 0)])  4.43 us
  transfers between devices with their start and end apart: 24, of which 14 were waited for; matrix products, arithmetic and copies ran while one was open for 5% of the time, Pallas kernels for 8%

profile of v3, /device:TPU:0, one launch (start us, length us, event | category | flops | bytes accessed | tf_op | source)
XLA Modules:
  0.0 196.5 jit_solution(13933993367182527700)
XLA Ops:
  1.6 2.9 %collective-permute-start.3 = (bf16[2,384,128]{2,1,0:T(8,128)(2,1)S(1)}, bf16[2,384,128]{2,1,0:T(8,128)(2,1)S(1)}, u32[]{:S(2)}, u32[]{:S(2)}) collective-permute-start(bf16[2,384,128]{2,1,0:T(8,128)(2,1)S(1)} %pad_maximum_fusion.4), channel_id=1, source_target_pairs={{0,24},{8,0},{16,8},{24,16},{32,40},{40,48},{48,56},{56,32},{1,25}... | collective-permute-start | bytes 589832 | tf_op jit(solution)/shard_map/ppermute | solution.py:36
  12.1 2.5 %copy-done = bf16[128,128,128]{2,1,0:T(8,128)(2,1)S(1)} copy-done((bf16[128,128,128]{2,1,0:T(8,128)(2,1)S(1)}, bf16[128,128,128]{2,1,0:T(8,128)(2,1)}, u32[]{:S(2)}) %copy-start) | copy-done | bytes 4194328
  14.6 2.2 %copy-done.1 = bf16[128,128,128]{2,1,0:T(8,128)(2,1)S(1)} copy-done((bf16[128,128,128]{2,1,0:T(8,128)(2,1)S(1)}, bf16[128,128,128]{2,1,0:T(8,128)(2,1)}, u32[]{:S(2)}) %copy-start.1) | copy-done | bytes 4194328
  16.8 3.6 %terms.4 = bf16[8,384,256]{2,1,0:T(8,128)(2,1)S(1)} custom-call(s32[256]{0:T(256)S(1)} %select_reduce_fusion.tab, s32[32]{0:T(128)S(1)} %mul.220.order, bf16[384,1024]{1,0:T(8,128)(2,1)S(1)} %get-tuple-element.25.gu, bf16[128,128,128]{2,1,0:T(8,128)(2,1)S(1)} %copy-done, bf16[128,128,128]{2,1,0:T(8,128)(2,1)S(1)} %copy-done.1), custom_call_target="tpu_custom_call" | custom-call | flops 1610612736 | bytes 10485760 | tf_op jit(solution)/shard_map/terms/pallas_call | solution.py:93
  22.4 2.0 %collective-permute-start.5 = (bf16[4,384,128]{2,1,0:T(8,128)(2,1)S(1)}, bf16[4,384,128]{2,1,0:T(8,128)(2,1)S(1)}, u32[]{:S(2)}, u32[]{:S(2)}) collective-permute-start(bf16[4,384,128]{2,1,0:T(8,128)(2,1)S(1)} %get-tuple-element.22), channel_id=1, source_target_pairs={{0,2},{2,4},{4,6},{6,0},{32,38},{34,32},{36,34},{38,36},{1,3},{3,5... | collective-permute-start | bytes 1179656 | tf_op jit(solution)/shard_map/ppermute | solution.py:36
  24.4 3.2 %collective-permute-start.14 = (bf16[1024,384]{1,0:T(8,128)(2,1)S(1)}, bf16[1024,384]{1,0:T(8,128)(2,1)S(1)}, u32[]{:S(2)}, u32[]{:S(2)}) collective-permute-start(bf16[1024,384]{1,0:T(8,128)(2,1)S(1)} %get-tuple-element.30.own_ref), channel_id=1, source_target_pairs={{0,64},{64,0},{1,65},{65,1},{2,66},{66,2},{3,67},{67,3},{4,68},{68... | collective-permute-start | bytes 2359304 | tf_op jit(solution)/shard_map/ppermute | solution.py:24
  28.3 3.6 %terms.5 = bf16[8,384,256]{2,1,0:T(8,128)(2,1)S(1)} custom-call(s32[256]{0:T(256)S(1)} %select_reduce_fusion.tab, s32[32]{0:T(128)S(1)} %mul.220.order, bf16[384,1024]{1,0:T(8,128)(2,1)S(1)} %get-tuple-element.25.gu, bf16[128,128,128]{2,1,0:T(8,128)(2,1)S(1)} %copy-done, bf16[128,128,128]{2,1,0:T(8,128)(2,1)S(1)} %copy-done.1), custom_call_target="tpu_custom_call" | custom-call | flops 1610612736 | bytes 10485760 | tf_op jit(solution)/shard_map/terms/pallas_call | solution.py:93
  33.9 16.0 %collective-permute-done.6 = bf16[4,384,128]{2,1,0:T(8,128)(2,1)S(1)} collective-permute-done((bf16[4,384,128]{2,1,0:T(8,128)(2,1)S(1)}, bf16[4,384,128]{2,1,0:T(8,128)(2,1)S(1)}, u32[]{:S(2)}, u32[]{:S(2)}) %collective-permute-start.6) | collective-permute-done | bytes 393248 | tf_op jit(solution)/shard_map/ppermute | solution.py:36
  51.6 3.6 %terms.6 = bf16[8,384,256]{2,1,0:T(8,128)(2,1)S(1)} custom-call(s32[256]{0:T(256)S(1)} %select_reduce_fusion.tab, s32[32]{0:T(128)S(1)} %mul.220.order, bf16[384,1024]{1,0:T(8,128)(2,1)S(1)} %get-tuple-element.25.gu, bf16[128,128,128]{2,1,0:T(8,128)(2,1)S(1)} %copy-done, bf16[128,128,128]{2,1,0:T(8,128)(2,1)S(1)} %copy-done.1), custom_call_target="tpu_custom_call" | custom-call | flops 1610612736 | bytes 10485760 | tf_op jit(solution)/shard_map/terms/pallas_call | solution.py:93
  56.8 2.0 %collective-permute-done.9 = bf16[4,384,128]{2,1,0:T(8,128)(2,1)S(1)} collective-permute-done((bf16[4,384,128]{2,1,0:T(8,128)(2,1)S(1)}, bf16[4,384,128]{2,1,0:T(8,128)(2,1)S(1)}, u32[]{:S(2)}, u32[]{:S(2)}) %collective-permute-start.9) | collective-permute-done | bytes 393248 | tf_op jit(solution)/shard_map/ppermute | solution.py:36
  59.4 3.6 %terms.7 = bf16[8,384,256]{2,1,0:T(8,128)(2,1)S(1)} custom-call(s32[256]{0:T(256)S(1)} %select_reduce_fusion.tab, s32[32]{0:T(128)S(1)} %mul.220.order, bf16[384,1024]{1,0:T(8,128)(2,1)S(1)} %get-tuple-element.25.gu, bf16[128,128,128]{2,1,0:T(8,128)(2,1)S(1)} %copy-done, bf16[128,128,128]{2,1,0:T(8,128)(2,1)S(1)} %copy-done.1), custom_call_target="tpu_custom_call" | custom-call | flops 1610612736 | bytes 10485760 | tf_op jit(solution)/shard_map/terms/pallas_call | solution.py:93
  64.5 3.3 %collective-permute-done.19 = bf16[4,384,128]{2,1,0:T(8,128)(2,1)S(1)} collective-permute-done((bf16[4,384,128]{2,1,0:T(8,128)(2,1)S(1)}, bf16[4,384,128]{2,1,0:T(8,128)(2,1)S(1)}, u32[]{:S(2)}, u32[]{:S(2)}) %collective-permute-start.19) | collective-permute-done | bytes 393248 | tf_op jit(solution)/shard_map/ppermute | solution.py:36
  68.2 9.5 %collective-permute-done.4 = bf16[8,384,256]{2,1,0:T(8,128)(2,1)S(1)} collective-permute-done((bf16[8,384,256]{2,1,0:T(8,128)(2,1)S(1)}, bf16[8,384,256]{2,1,0:T(8,128)(2,1)S(1)}, u32[]{:S(2)}, u32[]{:S(2)}) %collective-permute-start.4) | collective-permute-done | bytes 1572896 | tf_op jit(solution)/shard_map/ppermute | solution.py:36
  78.2 11.5 %collective-permute-done.20.rest_5_ = bf16[16,384,128]{2,1,0:T(8,128)(2,1)S(1)} collective-permute-done((bf16[16,384,128]{2,1,0:T(8,128)(2,1)S(1)}, bf16[16,384,128]{2,1,0:T(8,128)(2,1)S(1)}, u32[]{:S(2)}, u32[]{:S(2)}) %collective-permute-start.20) | collective-permute-done | bytes 1572896 | tf_op jit(solution)/shard_map/ppermute | solution.py:36
  90.9 8.9 %collective-permute-done.7 = bf16[8,384,256]{2,1,0:T(8,128)(2,1)S(1)} collective-permute-done((bf16[8,384,256]{2,1,0:T(8,128)(2,1)S(1)}, bf16[8,384,256]{2,1,0:T(8,128)(2,1)S(1)}, u32[]{:S(2)}, u32[]{:S(2)}) %collective-permute-start.7) | collective-permute-done | bytes 1572896 | tf_op jit(solution)/shard_map/ppermute | solution.py:36
  101.4 10.2 %collective-permute-done.21.rest_6_ = bf16[16,384,128]{2,1,0:T(8,128)(2,1)} collective-permute-done((bf16[16,384,128]{2,1,0:T(8,128)(2,1)S(1)}, bf16[16,384,128]{2,1,0:T(8,128)(2,1)}, u32[]{:S(2)}, u32[]{:S(2)}) %collective-permute-start.21) | collective-permute-done | bytes 1572896 | tf_op jit(solution)/shard_map/ppermute | solution.py:36
  117.2 21.2 %collective-permute-done.10 = bf16[2,384,256]{2,1,0:T(8,128)(2,1)} collective-permute-done((bf16[2,384,256]{2,1,0:T(8,128)(2,1)S(1)}, bf16[2,384,256]{2,1,0:T(8,128)(2,1)}, u32[]{:S(2)}, u32[]{:S(2)}) %collective-permute-start.10) | collective-permute-done | bytes 393248 | tf_op jit(solution)/shard_map/ppermute | solution.py:36
  144.7 14.5 %wgrad.1 = bf16[128,256,128]{2,1,0:T(8,128)(2,1)} custom-call(s32[144]{0:T(256)S(1)} %get-tuple-element.41.lrow, s32[144]{0:T(256)S(1)} %get-tuple-element.40.lslot, s32[288]{0:T(512)S(1)} %reshape.594.lact, s32[3]{0:T(128)S(1)} %pad_add_fusion.1.meta, bf16[1024,384]{1,0:T(8,128)(2,1)S(1)} %copy-done.10, bf16[1024,384]{1,0:T(8,128)(2,1)S(1)} %copy-done.12, ...), custom_call_target="tpu_custom_call" | custom-call | flops 6442450944 | bytes 23068672 | tf_op jit(solution)/shard_map/wgrad/pallas_call | solution.py:147
  159.3 3.7 %collective-permute-start.11 = (bf16[2,384,256]{2,1,0:T(8,128)(2,1)S(1)}, bf16[2,384,256]{2,1,0:T(8,128)(2,1)S(1)}, u32[]{:S(2)}, u32[]{:S(2)}) collective-permute-start(bf16[2,384,256]{2,1,0:T(8,128)(2,1)S(1)} %add_convert_fusion.5), channel_id=1, source_target_pairs={{0,2},{2,4},{4,6},{6,0},{32,38},{34,32},{36,34},{38,36},{1,3},{3,5... | collective-permute-start | bytes 1179656 | tf_op jit(solution)/shard_map/ppermute | solution.py:36
  163.0 8.6 %collective-permute-done.11 = bf16[2,384,256]{2,1,0:T(8,128)(2,1)S(1)} collective-permute-done((bf16[2,384,256]{2,1,0:T(8,128)(2,1)S(1)}, bf16[2,384,256]{2,1,0:T(8,128)(2,1)S(1)}, u32[]{:S(2)}, u32[]{:S(2)}) %collective-permute-start.11) | collective-permute-done | bytes 393248 | tf_op jit(solution)/shard_map/ppermute | solution.py:36
  171.7 9.0 %collective-permute-done.12 = bf16[2,384,256]{2,1,0:T(8,128)(2,1)S(1)} collective-permute-done((bf16[2,384,256]{2,1,0:T(8,128)(2,1)S(1)}, bf16[2,384,256]{2,1,0:T(8,128)(2,1)S(1)}, u32[]{:S(2)}, u32[]{:S(2)}) %collective-permute-start.12) | collective-permute-done | bytes 393248 | tf_op jit(solution)/shard_map/ppermute | solution.py:36
  182.1 4.4 %collective-permute-done.13 = bf16[384,256]{1,0:T(8,128)(2,1)S(1)} collective-permute-done((bf16[384,256]{1,0:T(8,128)(2,1)S(1)}, bf16[384,256]{1,0:T(8,128)(2,1)S(1)}, u32[]{:S(2)}, u32[]{:S(2)}) %collective-permute-start.13) | collective-permute-done | bytes 196640 | tf_op jit(solution)/shard_map/ppermute | solution.py:24
  187.3 5.6 %add_convert_fusion = bf16[128,256,128]{2,1,0:T(8,128)(2,1)S(1)} fusion(bf16[128,256,128]{2,1,0:T(8,128)(2,1)S(1)} %collective-permute-done.23, bf16[128,256,128]{2,1,0:T(8,128)(2,1)} %wgrad.1), kind=kLoop, calls=%fused_computation | loop fusion | flops 16777216 | bytes 25165824 | tf_op jit(solution)/shard_map/convert_element_type | solution.py:40
  192.9 3.7 %fusion.13 = (bf16[128,128,128]{2,1,0:T(8,128)(2,1)}, bf16[128,128,128]{2,1,0:T(8,128)(2,1)}) fusion(bf16[128,256,128]{2,1,0:T(8,128)(2,1)S(1)} %add_convert_fusion), kind=kLoop, calls=%fused_computation.95 | loop fusion | bytes 16777216 | tf_op jit(solution)/shard_map/slice | solution.py:269
  (106 shorter events, 35.7 us)
Async XLA Ops:
  1.6 20.6 %collective-permute-start.3 = (bf16[2,384,128]{2,1,0:T(8,128)(2,1)S(1)}, bf16[2,384,128]{2,1,0:T(8,128)(2,1)S(1)}, u32[]{:S(2)}, u32[]{:S(2)}) collective-permute-start(bf16[2,384,128]{2,1,0:T(8,128)(2,1)S(1)} %pad_maximum_fusion.4), channel_id=1, source_target_pairs={{0,24},{8,0},{16,8},{24,16},{32,40},{40,48},{48,56},{56,32},{1,25}... | collective-permute-start | bytes 589832 | tf_op jit(solution)/shard_map/ppermute | solution.py:36
  4.5 17.7 %collective-permute-start.2 = (bf16[2,384,128]{2,1,0:T(8,128)(2,1)S(1)}, bf16[2,384,128]{2,1,0:T(8,128)(2,1)S(1)}, u32[]{:S(2)}, u32[]{:S(2)}) collective-permute-start(bf16[2,384,128]{2,1,0:T(8,128)(2,1)S(1)} %pad_maximum_fusion.4), channel_id=1, source_target_pairs={{0,16},{8,24},{16,0},{24,8},{32,48},{40,56},{48,32},{56,40},{1,17}... | collective-permute-start | bytes 589832 | tf_op jit(solution)/shard_map/ppermute | solution.py:36
  5.3 17.0 %collective-permute-start.1 = (bf16[2,384,128]{2,1,0:T(8,128)(2,1)S(1)}, bf16[2,384,128]{2,1,0:T(8,128)(2,1)S(1)}, u32[]{:S(2)}, u32[]{:S(2)}) collective-permute-start(bf16[2,384,128]{2,1,0:T(8,128)(2,1)S(1)} %pad_maximum_fusion.4), channel_id=1, source_target_pairs={{0,8},{8,16},{16,24},{24,0},{32,56},{40,32},{48,40},{56,48},{1,9},... | collective-permute-start | bytes 589832 | tf_op jit(solution)/shard_map/ppermute | solution.py:36
  20.4 34.9 %collective-permute-start = (bf16[8,384,256]{2,1,0:T(8,128)(2,1)S(1)}, bf16[8,384,256]{2,1,0:T(8,128)(2,1)S(1)}, u32[]{:S(2)}, u32[]{:S(2)}) collective-permute-start(bf16[8,384,256]{2,1,0:T(8,128)(2,1)S(1)} %terms.4), channel_id=1, source_target_pairs={{0,8},{8,16},{16,24},{24,0},{32,56},{40,32},{48,40},{56,48},{1,9},... | collective-permute-start | bytes 4718600 | tf_op jit(solution)/shard_map/ppermute | solution.py:36
  22.4 9.9 %collective-permute-start.5 = (bf16[4,384,128]{2,1,0:T(8,128)(2,1)S(1)}, bf16[4,384,128]{2,1,0:T(8,128)(2,1)S(1)}, u32[]{:S(2)}, u32[]{:S(2)}) collective-permute-start(bf16[4,384,128]{2,1,0:T(8,128)(2,1)S(1)} %get-tuple-element.22), channel_id=1, source_target_pairs={{0,2},{2,4},{4,6},{6,0},{32,38},{34,32},{36,34},{38,36},{1,3},{3,5... | collective-permute-start | bytes 1179656 | tf_op jit(solution)/shard_map/ppermute | solution.py:36
  24.4 30.8 %collective-permute-start.14 = (bf16[1024,384]{1,0:T(8,128)(2,1)S(1)}, bf16[1024,384]{1,0:T(8,128)(2,1)S(1)}, u32[]{:S(2)}, u32[]{:S(2)}) collective-permute-start(bf16[1024,384]{1,0:T(8,128)(2,1)S(1)} %get-tuple-element.30.own_ref), channel_id=1, source_target_pairs={{0,64},{64,0},{1,65},{65,1},{2,66},{66,2},{3,67},{67,3},{4,68},{68... | collective-permute-start | bytes 2359304 | tf_op jit(solution)/shard_map/ppermute | solution.py:24
  27.6 22.2 %collective-permute-start.6 = (bf16[4,384,128]{2,1,0:T(8,128)(2,1)S(1)}, bf16[4,384,128]{2,1,0:T(8,128)(2,1)S(1)}, u32[]{:S(2)}, u32[]{:S(2)}) collective-permute-start(bf16[4,384,128]{2,1,0:T(8,128)(2,1)S(1)} %get-tuple-element.23), channel_id=1, source_target_pairs={{0,1},{1,64},{32,97},{33,32},{64,65},{65,0},{96,33},{97,96},{2,3},... | collective-permute-start | bytes 1179656 | tf_op jit(solution)/shard_map/ppermute | solution.py:36
  32.3 22.9 %collective-permute-start.8 = (bf16[4,384,128]{2,1,0:T(8,128)(2,1)S(1)}, bf16[4,384,128]{2,1,0:T(8,128)(2,1)S(1)}, u32[]{:S(2)}, u32[]{:S(2)}) collective-permute-start(bf16[4,384,128]{2,1,0:T(8,128)(2,1)S(1)} %collective-permute-done.5), channel_id=1, source_target_pairs={{0,2},{2,4},{4,6},{6,0},{32,38},{34,32},{36,34},{38,36},{1,3},{3,5... | collective-permute-start | bytes 1179656 | tf_op jit(solution)/shard_map/ppermute | solution.py:36
  49.9 9.0 %collective-permute-start.9 = (bf16[4,384,128]{2,1,0:T(8,128)(2,1)S(1)}, bf16[4,384,128]{2,1,0:T(8,128)(2,1)S(1)}, u32[]{:S(2)}, u32[]{:S(2)}) collective-permute-start(bf16[4,384,128]{2,1,0:T(8,128)(2,1)S(1)} %collective-permute-done.6), channel_id=1, source_target_pairs={{0,1},{1,64},{32,97},{33,32},{64,65},{65,0},{96,33},{97,96},{2,3},... | collective-permute-start | bytes 1179656 | tf_op jit(solution)/shard_map/ppermute | solution.py:36
  55.2 9.1 %collective-permute-start.15 = (bf16[4,384,128]{2,1,0:T(8,128)(2,1)S(1)}, bf16[4,384,128]{2,1,0:T(8,128)(2,1)S(1)}, u32[]{:S(2)}, u32[]{:S(2)}) collective-permute-start(bf16[4,384,128]{2,1,0:T(8,128)(2,1)S(1)} %collective-permute-done.8), channel_id=1, source_target_pairs={{0,2},{2,4},{4,6},{6,0},{32,38},{34,32},{36,34},{38,36},{1,3},{3,5... | collective-permute-start | bytes 1179656 | tf_op jit(solution)/shard_map/ppermute | solution.py:36
  56.1 21.6 %collective-permute-start.4 = (bf16[8,384,256]{2,1,0:T(8,128)(2,1)S(1)}, bf16[8,384,256]{2,1,0:T(8,128)(2,1)S(1)}, u32[]{:S(2)}, u32[]{:S(2)}) collective-permute-start(bf16[8,384,256]{2,1,0:T(8,128)(2,1)S(1)} %add_convert_fusion.3), channel_id=1, source_target_pairs={{0,8},{8,16},{16,24},{24,0},{32,56},{40,32},{48,40},{56,48},{1,9},... | collective-permute-start | bytes 4718600 | tf_op jit(solution)/shard_map/ppermute | solution.py:36
  58.9 9.0 %collective-permute-start.19 = (bf16[4,384,128]{2,1,0:T(8,128)(2,1)S(1)}, bf16[4,384,128]{2,1,0:T(8,128)(2,1)S(1)}, u32[]{:S(2)}, u32[]{:S(2)}) collective-permute-start(bf16[4,384,128]{2,1,0:T(8,128)(2,1)S(1)} %collective-permute-done.9), channel_id=1, source_target_pairs={{0,1},{1,64},{32,97},{33,32},{64,65},{65,0},{96,33},{97,96},{2,3},... | collective-permute-start | bytes 1179656 | tf_op jit(solution)/shard_map/ppermute | solution.py:36
  68.0 21.7 %collective-permute-start.20 = (bf16[16,384,128]{2,1,0:T(8,128)(2,1)S(1)}, bf16[16,384,128]{2,1,0:T(8,128)(2,1)S(1)}, u32[]{:S(2)}, u32[]{:S(2)}) collective-permute-start(bf16[16,384,128]{2,1,0:T(8,128)(2,1)S(1)} %pad_maximum_fusion.1.rest_4_), channel_id=1, source_target_pairs={{0,2},{2,4},{4,6},{6,0},{32,38},{34,32},{36,34},{38,36},{1,3},{3,5... | collective-permute-start | bytes 4718600 | tf_op jit(solution)/shard_map/ppermute | solution.py:36
  68.1 21.7 %collective-permute-start.16 = (bf16[16,384,128]{2,1,0:T(8,128)(2,1)S(1)}, bf16[16,384,128]{2,1,0:T(8,128)(2,1)S(1)}, u32[]{:S(2)}, u32[]{:S(2)}) collective-permute-start(bf16[16,384,128]{2,1,0:T(8,128)(2,1)S(1)} %pad_maximum_fusion.rest_0_), channel_id=1, source_target_pairs={{0,1},{1,64},{32,97},{33,32},{64,65},{65,0},{96,33},{97,96},{2,3},... | collective-permute-start | bytes 4718600 | tf_op jit(solution)/shard_map/ppermute | solution.py:36
  78.1 21.7 %collective-permute-start.7 = (bf16[8,384,256]{2,1,0:T(8,128)(2,1)S(1)}, bf16[8,384,256]{2,1,0:T(8,128)(2,1)S(1)}, u32[]{:S(2)}, u32[]{:S(2)}) collective-permute-start(bf16[8,384,256]{2,1,0:T(8,128)(2,1)S(1)} %add_convert_fusion.2), channel_id=1, source_target_pairs={{0,8},{8,16},{16,24},{24,0},{32,56},{40,32},{48,40},{56,48},{1,9},... | collective-permute-start | bytes 4718600 | tf_op jit(solution)/shard_map/ppermute | solution.py:36
  89.8 21.8 %collective-permute-start.17 = (bf16[16,384,128]{2,1,0:T(8,128)(2,1)S(1)}, bf16[16,384,128]{2,1,0:T(8,128)(2,1)}, u32[]{:S(2)}, u32[]{:S(2)}) collective-permute-start(bf16[16,384,128]{2,1,0:T(8,128)(2,1)S(1)} %collective-permute-done.16.rest_1_), channel_id=1, source_target_pairs={{0,1},{1,64},{32,97},{33,32},{64,65},{65,0},{96,33},{97,96},{2,3},... | collective-permute-start | bytes 4718600 | tf_op jit(solution)/shard_map/ppermute | solution.py:36
  89.8 21.8 %collective-permute-start.21 = (bf16[16,384,128]{2,1,0:T(8,128)(2,1)S(1)}, bf16[16,384,128]{2,1,0:T(8,128)(2,1)}, u32[]{:S(2)}, u32[]{:S(2)}) collective-permute-start(bf16[16,384,128]{2,1,0:T(8,128)(2,1)S(1)} %collective-permute-done.20.rest_5_), channel_id=1, source_target_pairs={{0,2},{2,4},{4,6},{6,0},{32,38},{34,32},{36,34},{38,36},{1,3},{3,5... | collective-permute-start | bytes 4718600 | tf_op jit(solution)/shard_map/ppermute | solution.py:36
  111.6 27.9 %collective-permute-start.18 = (bf16[16,384,128]{2,1,0:T(8,128)(2,1)}, bf16[16,384,128]{2,1,0:T(8,128)(2,1)}, u32[]{:S(2)}, u32[]{:S(2)}) collective-permute-start(bf16[16,384,128]{2,1,0:T(8,128)(2,1)} %collective-permute-done.17.rest_2_), channel_id=1, source_target_pairs={{0,1},{1,64},{32,97},{33,32},{64,65},{65,0},{96,33},{97,96},{2,3},... | collective-permute-start | bytes 4718600 | tf_op jit(solution)/shard_map/ppermute | solution.py:36
  112.2 27.4 %collective-permute-start.22 = (bf16[16,384,128]{2,1,0:T(8,128)(2,1)}, bf16[16,384,128]{2,1,0:T(8,128)(2,1)}, u32[]{:S(2)}, u32[]{:S(2)}) collective-permute-start(bf16[16,384,128]{2,1,0:T(8,128)(2,1)} %collective-permute-done.21.rest_6_), channel_id=1, source_target_pairs={{0,2},{2,4},{4,6},{6,0},{32,38},{34,32},{36,34},{38,36},{1,3},{3,5... | collective-permute-start | bytes 4718600 | tf_op jit(solution)/shard_map/ppermute | solution.py:36
  113.5 24.9 %collective-permute-start.10 = (bf16[2,384,256]{2,1,0:T(8,128)(2,1)S(1)}, bf16[2,384,256]{2,1,0:T(8,128)(2,1)}, u32[]{:S(2)}, u32[]{:S(2)}) collective-permute-start(bf16[2,384,256]{2,1,0:T(8,128)(2,1)S(1)} %slice.77), channel_id=1, source_target_pairs={{0,2},{2,4},{4,6},{6,0},{32,38},{34,32},{36,34},{38,36},{1,3},{3,5... | collective-permute-start | bytes 1179656 | tf_op jit(solution)/shard_map/ppermute | solution.py:36
  159.2 28.1 %collective-permute-start.23 = (bf16[128,256,128]{2,1,0:T(8,128)(2,1)}, bf16[128,256,128]{2,1,0:T(8,128)(2,1)S(1)}, u32[]{:S(2)}, u32[]{:S(2)}) collective-permute-start(bf16[128,256,128]{2,1,0:T(8,128)(2,1)} %wgrad.1), channel_id=1, source_target_pairs={{0,32},{32,0},{1,33},{33,1},{2,34},{34,2},{3,35},{35,3},{4,36},{36... | collective-permute-start | bytes 25165832 | tf_op jit(solution)/shard_map/ppermute | solution.py:24
  159.3 12.3 %collective-permute-start.11 = (bf16[2,384,256]{2,1,0:T(8,128)(2,1)S(1)}, bf16[2,384,256]{2,1,0:T(8,128)(2,1)S(1)}, u32[]{:S(2)}, u32[]{:S(2)}) collective-permute-start(bf16[2,384,256]{2,1,0:T(8,128)(2,1)S(1)} %add_convert_fusion.5), channel_id=1, source_target_pairs={{0,2},{2,4},{4,6},{6,0},{32,38},{34,32},{36,34},{38,36},{1,3},{3,5... | collective-permute-start | bytes 1179656 | tf_op jit(solution)/shard_map/ppermute | solution.py:36
  171.7 9.1 %collective-permute-start.12 = (bf16[2,384,256]{2,1,0:T(8,128)(2,1)S(1)}, bf16[2,384,256]{2,1,0:T(8,128)(2,1)S(1)}, u32[]{:S(2)}, u32[]{:S(2)}) collective-permute-start(bf16[2,384,256]{2,1,0:T(8,128)(2,1)S(1)} %add_convert_fusion.4), channel_id=1, source_target_pairs={{0,2},{2,4},{4,6},{6,0},{32,38},{34,32},{36,34},{38,36},{1,3},{3,5... | collective-permute-start | bytes 1179656 | tf_op jit(solution)/shard_map/ppermute | solution.py:36
  180.8 5.7 %collective-permute-start.13 = (bf16[384,256]{1,0:T(8,128)(2,1)S(1)}, bf16[384,256]{1,0:T(8,128)(2,1)S(1)}, u32[]{:S(2)}, u32[]{:S(2)}) collective-permute-start(bf16[384,256]{1,0:T(8,128)(2,1)S(1)} %fusion), channel_id=1, source_target_pairs={{0,1},{1,0},{2,3},{3,2},{4,5},{5,4},{6,7},{7,6},{8,9},{9,8},{10,11... | collective-permute-start | bytes 589832 | tf_op jit(solution)/shard_map/ppermute | solution.py:24
  (15 other events, 97.4 us)

commit v4 on v3

v4 whole, which is shorter than its diff:
```python
import functools

import jax
import jax.numpy as jnp
from jax import lax
from jax.experimental import pallas as pl
from jax.experimental.pallas import tpu as pltpu
from jax.sharding import Mesh
from jax.sharding import PartitionSpec as P

BF = jnp.bfloat16
F32 = jnp.float32
AXES = {"x": ("c", "x"), "z": ("c", "z"), "y": ("yh", "c", "yl")}
SIZES = {"yh": 2, "c": 2, "x": 4, "z": 4, "yl": 2}
TOK = 384
SLOTS = 128
PAIRS = 76


def shift(value, axis, step):
    pairs = []
    if axis in ("yh", "c", "yl"):
        return lax.ppermute(value, axis, [(0, 1), (1, 0)])
    if axis == "y":
        for yh in range(2):
            for c in range(2):
                for yl in range(2):
                    y = (yh * 2 + yl + (step if c == 0 else -step)) % 4
                    pairs.append(((yh * 2 + c) * 2 + yl, ((y // 2) * 2 + c) * 2 + y % 2))
    else:
        for c in range(2):
            for a in range(4):
                b = (a + (step if c == 0 else -step)) % 4
                pairs.append((c * 4 + a, c * 4 + b))
    return lax.ppermute(value, AXES[axis], pairs)


def add(a, b):
    return (a.astype(F32) + b.astype(F32)).astype(BF)


def gates_kernel(gate_ref, up_ref, hid_ref, gu, gut):
    g = gate_ref[...].astype(F32)
    u = up_ref[...].astype(F32)
    h = hid_ref[...].astype(F32)
    sig = 1.0 / (1.0 + jnp.exp(-g))
    gg = h * u * sig * (1.0 + g * (1.0 - sig))
    ug = h * g * sig
    gu[:, :128] = gg.astype(BF)
    gu[:, 128:] = ug.astype(BF)
    gut[:128, :] = gg.T.astype(BF)
    gut[128:, :] = ug.T.astype(BF)


def chunk_kernel(k, tab, order, gu, wg, wu, out):
    @pl.loop(0, 8)
    def _(j):
        base = order[k * 8 + j]
        total = jnp.zeros((TOK, 256), F32)
        for r in range(4):
            sides = []
            for side in range(2):
                slot = tab[r * 64 + base + side]
                index = jnp.minimum(slot, SLOTS - 1)
                block = jnp.concatenate([wg[index], wu[index]], axis=0)
                sides.append(jnp.where(slot < SLOTS, block, jnp.zeros_like(block)))
            both = jnp.concatenate(sides, axis=1)
            total += jnp.dot(gu[:, r * 256 : (r + 1) * 256], both, preferred_element_type=F32)
        out[j] = total.astype(BF)


PIECE = jax.ShapeDtypeStruct((8, TOK, 256), BF)
VM = pl.BlockSpec(memory_space=pltpu.VMEM)
SM = pl.BlockSpec(memory_space=pltpu.SMEM)
ANY = pl.BlockSpec(memory_space=pl.ANY)


def gates(gate_pre, up_pre, hidden):
    return pl.pallas_call(
        gates_kernel,
        out_shape=[jax.ShapeDtypeStruct((TOK, 1024), BF), jax.ShapeDtypeStruct((1024, TOK), BF)],
        grid=(4,),
        in_specs=[pl.BlockSpec((TOK, 128), lambda r: (0, r))] * 3,
        out_specs=[pl.BlockSpec((TOK, 256), lambda r: (0, r)), pl.BlockSpec((256, TOK), lambda r: (r, 0))],
        compiler_params=pltpu.CompilerParams(vmem_limit_bytes=16 * 1024 * 1024),
        cost_estimate=pl.CostEstimate(flops=TOK * 512 * 20, bytes_accessed=3 << 20, transcendentals=TOK * 512),
        name="gates",
    )(gate_pre, up_pre, hidden)


def terms(k, tab, order, gu, wg, wu):
    return pl.pallas_call(
        functools.partial(chunk_kernel, k),
        out_shape=PIECE,
        in_specs=[SM] * 2 + [VM] * 3,
        out_specs=VM,
        compiler_params=pltpu.CompilerParams(vmem_limit_bytes=24 * 1024 * 1024),
        cost_estimate=pl.CostEstimate(flops=2 * TOK * 1024 * 2048, bytes_accessed=10 << 20, transcendentals=0),
        name="terms",
    )(tab, order, gu, wg, wu)


def put(block, grads, slot, sem):
    pltpu.make_async_copy(block, grads.at[slot], sem).start()


def finish(copies, zero, grads, sem):
    @pl.loop(0, copies)
    def _(_):
        pltpu.make_async_copy(zero, grads.at[0], sem).wait()


def same_row_pairs(low, high, refs, groups, lrow, lslot, ltile, gt, gate, up, gbuf, ubuf, sem):
    @pl.loop(low, high)
    def _(p):
        pos = p * 2
        rows = pl.ds(pl.multiple_of(lrow[pos] * 256, 256), 256)
        left = jnp.concatenate([gt[g, rows, :] for g in groups], axis=1)
        sides = []
        for side in range(2):
            tiles = [ref[ltile[(pos + side) * 4 + n]] for n, ref in enumerate(refs)]
            sides.append(jnp.concatenate(tiles, axis=0))
        total = jnp.dot(left, jnp.concatenate(sides, axis=1), preferred_element_type=F32).astype(BF)
        for side in range(2):
            gbuf[pos + side] = total[:128, side * 128 : side * 128 + 128]
            ubuf[pos + side] = total[128:, side * 128 : side * 128 + 128]
        put(gbuf.at[pos], gate, lslot[pos], sem)
        put(ubuf.at[pos], up, lslot[pos], sem)

        @pl.when(lslot[pos + 1] < SLOTS)
        def _():
            put(gbuf.at[pos + 1], gate, lslot[pos + 1], sem)
            put(ubuf.at[pos + 1], up, lslot[pos + 1], sem)


def early_kernel(
    lrow, lslot, ltile, meta, gt, e0, e2, o0, o2, e0c, e2c, o0c, o2c, gate, up, gbuf, ubuf, zero, sem
):
    zero[...] = jnp.zeros((128, 128), BF)

    @pl.loop(meta[8], SLOTS)
    def _(s):
        put(zero, gate, s, sem)
        put(zero, up, s, sem)

    lists = (lrow, lslot, ltile, gt, gate, up, gbuf, ubuf, sem)
    same_row_pairs(meta[0], meta[1], (e0, e2, e0c, e2c), (0, 1, 2, 3), *lists)
    same_row_pairs(meta[1], meta[2], (o0, o0, o0c, o0c), (0, 1, 2, 3), *lists)
    same_row_pairs(meta[2], meta[3], (o2, o2, o2c, o2c), (0, 1, 2, 3), *lists)
    finish(2 * (SLOTS - meta[9]), zero, gate, sem)


def late_kernel(
    lrow, lslot, ltile, meta, gt, e1, e3, o1, o3, e1c, e3c, o1c, o3c, gate_in, up_in, gate, up, gbuf, ubuf, zero, sem
):
    del gate_in, up_in
    lists = (lrow, lslot, ltile, gt, gate, up, gbuf, ubuf, sem)
    flip = meta[7]
    same_row_pairs(meta[3], meta[4], (e1, e3, e1c, e3c), (flip, 1 - flip, 3 - flip, 2 + flip), *lists)
    same_row_pairs(meta[4], meta[5], (o3, o3, o1c, o1c), (0, 1, 2, 3), *lists)
    same_row_pairs(meta[5], meta[6], (o1, o1, o3c, o3c), (0, 1, 2, 3), *lists)
    finish(2 * meta[9], zero, gate, sem)


def weight_grads(kernel, name, lists, gt, pieces, held=()):
    grads = jax.ShapeDtypeStruct((SLOTS, 128, 128), BF)
    return pl.pallas_call(
        kernel,
        out_shape=[grads] * 2,
        in_specs=[SM] * 4 + [VM] * 9 + [ANY] * len(held),
        out_specs=[ANY] * 2,
        scratch_shapes=[
            pltpu.VMEM((2 * PAIRS, 128, 128), BF),
            pltpu.VMEM((2 * PAIRS, 128, 128), BF),
            pltpu.VMEM((128, 128), BF),
            pltpu.SemaphoreType.DMA,
        ],
        input_output_aliases={13 + n: n for n in range(len(held))},
        compiler_params=pltpu.CompilerParams(vmem_limit_bytes=24 * 1024 * 1024),
        cost_estimate=pl.CostEstimate(flops=2 * 1536 * 256 * 128 * 64, bytes_accessed=22 << 20, transcendentals=0),
        name=name,
    )(*lists, gt, *pieces, *held)


def tables(block_rows, block_cols, block_count):
    i32 = jnp.int32
    x, z = lax.axis_index("x"), lax.axis_index("z")
    yh, yl = lax.axis_index("yh"), lax.axis_index("yl")
    sign = 1 - 2 * lax.axis_index("c")
    slots = jnp.arange(SLOTS, dtype=i32)
    live = slots < block_count[0]
    row = block_rows % 4
    col = block_cols
    key = jnp.where(live, row * 64 + col, -1)
    hit = key[None, :] == jnp.arange(256, dtype=i32)[:, None]
    tab = jnp.min(jnp.where(hit, slots[None, :], SLOTS), axis=1)
    k = jnp.arange(4, dtype=i32)
    xs = (x - sign * k) % 4
    zs = (z - sign * k) % 4
    ys = yl ^ jnp.arange(2, dtype=i32)
    order = (((xs[:, None, None] * 4 + zs[None, :, None]) * 2 + ys[None, None, :]) * 2).reshape(32)
    near = (sign * (z - (col >> 2))) % 4
    odd_kind = jnp.where(near == 0, 1, jnp.where(near == 2, 2, jnp.where(near == 3, 4, 5)))
    even_kind = jnp.where(((col >> 1) & 1) == yl, 0, 3)
    group = jnp.where((col & 1) == 0, even_kind, odd_kind) * 4 + row
    same = (group[:, None] == group[None, :]) & live[None, :]
    rank = jnp.sum(jnp.where(same & (slots[None, :] < slots[:, None]), 1, 0), axis=1)
    groups = jnp.arange(24, dtype=i32)
    count = jnp.sum(jnp.where((group[None, :] == groups[:, None]) & live[None, :], 1, 0), axis=1)
    npair = (count + 1) // 2
    edges = jnp.arange(7, dtype=i32) * 4
    bounds = jnp.sum(jnp.where(groups[None, :] < edges[:, None], npair[None, :], 0), axis=1)
    start = jnp.sum(jnp.where(groups[None, :] < group[:, None], npair[None, :], 0), axis=1)
    place = jnp.where(live, start * 2 + rank, -1)
    at = place[None, :] == jnp.arange(2 * PAIRS, dtype=i32)[:, None]
    lslot = jnp.min(jnp.where(at, slots[None, :], SLOTS), axis=1)
    lrow = jnp.sum(jnp.where(at, row[None, :], 0), axis=1)
    lcol = jnp.sum(jnp.where(at, col[None, :], 0), axis=1)
    cx, cz, cy, par = lcol >> 4, (lcol >> 2) & 3, (lcol >> 1) & 1, lcol & 1
    tiles = []
    for way in (sign, -sign):
        kx = (way * (x - cx)) % 4
        kz = (way * (z - cz)) % 4
        for j in range(2):
            ky = (way * ((yh * 2 + yl) - ((yh ^ j) * 2 + cy))) % 4
            tiles.append(jnp.where(par == 0, kz, ky) * 4 + kx)
    ltile = jnp.stack(tiles, axis=1).reshape(-1)
    flip = jnp.where((yl == 1) == (sign == 1), 0, 1).astype(i32)
    late = jnp.sum(jnp.where(live & (group >= 12), 1, 0))
    meta = jnp.concatenate([bounds, flip[None], block_count, late[None]]).astype(i32)
    return tab, order, lrow, lslot, ltile, meta


def after(value, *others):
    return lax.optimization_barrier((value, *others))[0]


def body(
    activations, gate_pre, up_pre, hidden_grad, gate_blocks, up_blocks, block_rows, block_cols, block_count,
):
    tab, order, lrow, lslot, ltile, meta = tables(block_rows, block_cols, block_count)
    both = jnp.stack([activations[:, :128], activations[:, 128:]])
    near = [both] + [shift(both, "x", k) for k in (1, 2, 3)]
    gu, gut = gates(gate_pre, up_pre, hidden_grad)
    other = shift(gut, "yh", 1)
    t1 = terms(1, tab, order, gu, gate_blocks, up_blocks)
    moving = shift(t1, "x", 1)
    even = after(jnp.stack([v[0] for v in near]), t1)
    odd = after(jnp.stack([v[1] for v in near]), t1, other)
    evens, odds = [even], [odd]
    evens.append(shift(even, "z", 1))
    odds.append(shift(odd, "y", 1))
    t2 = terms(2, tab, order, after(gu, even, odd), gate_blocks, up_blocks)
    evens.append(shift(after(evens[1], t2), "z", 1))
    odds.append(shift(after(odds[1], t2), "y", 1))
    t3 = terms(3, tab, order, after(gu, evens[1], odds[1]), gate_blocks, up_blocks)
    moving = add(moving, t2)
    evens.append(shift(after(evens[2], t3), "z", 1))
    odds.append(shift(after(odds[2], t3), "y", 1))
    moving = shift(moving, "x", 1)
    t0 = terms(0, tab, order, after(gu, evens[2], odds[2]), gate_blocks, up_blocks)
    own = jnp.stack([gut, other])
    gt = jnp.concatenate([own, shift(own, "c", 1)])
    evens = [after(jnp.concatenate(evens), t0)]
    odds = [after(jnp.concatenate(odds), t0)]
    evens.append(shift(evens[0], "y", 1))
    odds.append(shift(odds[0], "z", 1))
    evens_c = [shift(evens[0], "c", 1)]
    odds_c = [shift(odds[0], "c", 1)]
    moving = add(moving, t3)
    evens.append(shift(after(evens[1], moving, gt), "y", 1))
    odds.append(shift(after(odds[1], moving, evens_c[0], odds_c[0]), "z", 1))
    moving = shift(moving, "x", 1)
    evens_c.append(shift(evens[1], "c", 1))
    odds_c.append(shift(odds[1], "c", 1))
    mine = add(moving, t0).reshape(4, 2, TOK, 256)
    evens.append(shift(after(evens[2], mine, evens_c[1]), "y", 1))
    odds.append(shift(after(odds[2], mine, odds_c[1]), "z", 1))
    evens_c.append(shift(evens[2], "c", 1))
    odds_c.append(shift(odds[2], "c", 1))
    moving = shift(mine[1], "z", 1)
    moving = add(moving, mine[2])
    early = [v[n] for v in (evens, odds, evens_c, odds_c) for n in (0, 2)]
    grads = weight_grads(
        early_kernel, "early_grads", (lrow, lslot, ltile, after(meta, moving)), gt, early
    )
    moving = add(after(shift(moving, "z", 1), grads[0]), mine[3])
    moving = shift(moving, "z", 1)
    keep = moving[0].astype(F32) + mine[0, 0].astype(F32)
    send = add(moving[1], mine[0, 1])
    evens_c.append(shift(after(evens[3], send), "c", 1))
    odds_c.append(shift(after(odds[3], send), "c", 1))
    input_grad = (keep + shift(send, "yl", 1).astype(F32)).astype(BF)
    late = [v[n] for v in (evens, odds, evens_c, odds_c) for n in (1, 3)]
    gate_grad, up_grad = weight_grads(
        late_kernel, "late_grads", (lrow, lslot, ltile, after(meta, input_grad)), gt, late, grads
    )
    return input_grad, gate_grad, up_grad


def solution(mesh):
    fine = Mesh(mesh.devices.reshape(2, 2, 4, 4, 2), ("yh", "c", "x", "z", "yl"))
    tok, wt = ("yh", "c"), ("x", "z", "yl")
    in_specs = (P(tok, wt),) * 4 + (P(wt, None, None),) * 2 + (P(wt),) * 3
    out_specs = (P(tok, wt), P(wt, None, None), P(wt, None, None))
    return jax.shard_map(body, mesh=fine, in_specs=in_specs, out_specs=out_specs, check_vma=False)
```

time: 199 us -> 173 us (0.87)
  waiting for transfers between devices: 106 us -> 62.5 us
  Pallas kernels: 30 us -> 42.3 us
  starting transfers between devices: 25.2 us -> 35.2 us
  other arithmetic: 12.6 us -> 9.95 us
    ppermute x21, waiting for transfers between devices: 102 us -> 53.6 us  [shift(): return lax.ppermute(value, AXES[axis], pairs)]
    pallas_call x1 -> x2, Pallas kernels: 14.5 us -> 26.8 us  [weight_grads(): pl.pallas_call(kernel, out_shape=[grads] * 2, in_specs=[SM] * 4 + [VM] *...]
    ppermute x3 -> x11, starting transfers between devices: 4.6 us -> 12.9 us  [shift(): return lax.ppermute(value, axis, [(0, 1), (1, 0)])]
    ppermute x3 -> x11, waiting for transfers between devices: 4.43 us -> 8.89 us  [shift(): return lax.ppermute(value, axis, [(0, 1), (1, 0)])]
    convert_element_type x7 -> x6, other arithmetic: 9.28 us -> 5.53 us  [add(): return (a.astype(F32) + b.astype(F32)).astype(BF)]
    slice x4 -> x3, local copies, waits for them, and re-layouts: 3.71 us -> 0.04 us  [body(): odd = after(jnp.stack([v[1] for v in near]), t1, other)]
    unnamed x30 -> x44, local copies, waits for them, and re-layouts: 13.1 us -> 16.5 us
  transfers between devices with their start and end apart: 24 -> 32, of which waited for: 14 -> 15; matrix products, arithmetic and copies ran while one was open for 5% -> 7% of each run, Pallas kernels for 8% -> 16%
where the time goes in v4:
time: 173 us; the launch traced here: 171 us
  waiting for transfers between devices  62.5 us (36%)
  Pallas kernels  42.3 us (24%)
  starting transfers between devices  35.2 us (20%)
  local copies, waits for them, and re-layouts  19.4 us (11%)
  other arithmetic  9.95 us (6%)
  between operations  1.92 us (1%)
    ppermute x21, waiting for transfers between devices, shift(): return lax.ppermute(value, AXES[axis], pairs)  53.6 us
    pallas_call x2, Pallas kernels, weight_grads(): pl.pallas_call(kernel, out_shape=[grads] * 2, in_specs=[SM] * 4 + [VM] *...  26.8 us
    ppermute x21, starting transfers between devices, shift(): return lax.ppermute(value, AXES[axis], pairs)  22.2 us
    unnamed x44, local copies, waits for them, and re-layouts  16.5 us
    pallas_call x4, Pallas kernels, terms(): pl.pallas_call(functools.partial(chunk_kernel, k), out_shape=PIECE, in_sp...  14.4 us
    ppermute x11, starting transfers between devices, shift(): return lax.ppermute(value, axis, [(0, 1), (1, 0)])  12.9 us
    ppermute x11, waiting for transfers between devices, shift(): return lax.ppermute(value, axis, [(0, 1), (1, 0)])  8.89 us
    convert_element_type x6, other arithmetic, add(): return (a.astype(F32) + b.astype(F32)).astype(BF)  5.53 us
  transfers between devices with their start and end apart: 32, of which 15 were waited for; matrix products, arithmetic and copies ran while one was open for 7% of the time, Pallas kernels for 16%

profile of v4, /device:TPU:0, one launch (start us, length us, event | category | flops | bytes accessed | tf_op | source)
XLA Modules:
  0.0 171.2 jit_solution(963720592977789975)
XLA Ops:
  1.6 2.9 %collective-permute-start.3 = (bf16[2,384,128]{2,1,0:T(8,128)(2,1)S(1)}, bf16[2,384,128]{2,1,0:T(8,128)(2,1)S(1)}, u32[]{:S(2)}, u32[]{:S(2)}) collective-permute-start(bf16[2,384,128]{2,1,0:T(8,128)(2,1)S(1)} %pad_maximum_fusion.6), channel_id=1, source_target_pairs={{0,24},{8,0},{16,8},{24,16},{32,40},{40,48},{48,56},{56,32},{1,25}... | collective-permute-start | bytes 589832 | tf_op jit(solution)/shard_map/ppermute | solution.py:35
  10.4 3.3 %collective-permute-start.4 = (bf16[1024,384]{1,0:T(8,128)(2,1)S(1)}, bf16[1024,384]{1,0:T(8,128)(2,1)S(1)}, u32[]{:S(2)}, u32[]{:S(2)}) collective-permute-start(bf16[1024,384]{1,0:T(8,128)(2,1)S(1)} %get-tuple-element.31), channel_id=1, source_target_pairs={{0,64},{64,0},{1,65},{65,1},{2,66},{66,2},{3,67},{67,3},{4,68},{68... | collective-permute-start | bytes 2359304 | tf_op jit(solution)/shard_map/ppermute | solution.py:23
  15.9 2.2 %copy-done = bf16[128,128,128]{2,1,0:T(8,128)(2,1)S(1)} copy-done((bf16[128,128,128]{2,1,0:T(8,128)(2,1)S(1)}, bf16[128,128,128]{2,1,0:T(8,128)(2,1)}, u32[]{:S(2)}) %copy-start) | copy-done | bytes 4194328
  18.1 2.2 %copy-done.1 = bf16[128,128,128]{2,1,0:T(8,128)(2,1)S(1)} copy-done((bf16[128,128,128]{2,1,0:T(8,128)(2,1)S(1)}, bf16[128,128,128]{2,1,0:T(8,128)(2,1)}, u32[]{:S(2)}) %copy-start.1) | copy-done | bytes 4194328
  20.3 3.6 %terms.4 = bf16[8,384,256]{2,1,0:T(8,128)(2,1)S(1)} custom-call(s32[256]{0:T(256)S(1)} %select_reduce_fusion.tab, s32[32]{0:T(128)S(1)} %mul.260.order, bf16[384,1024]{1,0:T(8,128)(2,1)S(1)} %get-tuple-element.34.gu, bf16[128,128,128]{2,1,0:T(8,128)(2,1)S(1)} %copy-done, bf16[128,128,128]{2,1,0:T(8,128)(2,1)S(1)} %copy-done.1), custom_call_target="tpu_custom_call" | custom-call | flops 1610612736 | bytes 10485760 | tf_op jit(solution)/shard_map/terms/pallas_call | solution.py:92
  27.9 3.7 %collective-permute-done.4 = bf16[1024,384]{1,0:T(8,128)(2,1)S(1)} collective-permute-done((bf16[1024,384]{1,0:T(8,128)(2,1)S(1)}, bf16[1024,384]{1,0:T(8,128)(2,1)S(1)}, u32[]{:S(2)}, u32[]{:S(2)}) %collective-permute-start.4) | collective-permute-done | bytes 786464 | tf_op jit(solution)/shard_map/ppermute | solution.py:23
  34.0 3.6 %terms.5 = bf16[8,384,256]{2,1,0:T(8,128)(2,1)S(1)} custom-call(s32[256]{0:T(256)S(1)} %select_reduce_fusion.tab, s32[32]{0:T(128)S(1)} %mul.260.order, bf16[384,1024]{1,0:T(8,128)(2,1)S(1)} %get-tuple-element.34.gu, bf16[128,128,128]{2,1,0:T(8,128)(2,1)S(1)} %copy-done, bf16[128,128,128]{2,1,0:T(8,128)(2,1)S(1)} %copy-done.1), custom_call_target="tpu_custom_call" | custom-call | flops 1610612736 | bytes 10485760 | tf_op jit(solution)/shard_map/terms/pallas_call | solution.py:92
  41.0 3.6 %terms.6 = bf16[8,384,256]{2,1,0:T(8,128)(2,1)S(1)} custom-call(s32[256]{0:T(256)S(1)} %select_reduce_fusion.tab, s32[32]{0:T(128)S(1)} %mul.260.order, bf16[384,1024]{1,0:T(8,128)(2,1)S(1)} %get-tuple-element.34.gu, bf16[128,128,128]{2,1,0:T(8,128)(2,1)S(1)} %copy-done, bf16[128,128,128]{2,1,0:T(8,128)(2,1)S(1)} %copy-done.1), custom_call_target="tpu_custom_call" | custom-call | flops 1610612736 | bytes 10485760 | tf_op jit(solution)/shard_map/terms/pallas_call | solution.py:92
  44.6 2.9 %collective-permute-done.9 = bf16[4,384,128]{2,1,0:T(8,128)(2,1)S(1)} collective-permute-done((bf16[4,384,128]{2,1,0:T(8,128)(2,1)S(1)}, bf16[4,384,128]{2,1,0:T(8,128)(2,1)S(1)}, u32[]{:S(2)}, u32[]{:S(2)}) %collective-permute-start.9) | collective-permute-done | bytes 393248 | tf_op jit(solution)/shard_map/ppermute | solution.py:35
  50.7 3.6 %terms.7 = bf16[8,384,256]{2,1,0:T(8,128)(2,1)S(1)} custom-call(s32[256]{0:T(256)S(1)} %select_reduce_fusion.tab, s32[32]{0:T(128)S(1)} %mul.260.order, bf16[384,1024]{1,0:T(8,128)(2,1)S(1)} %get-tuple-element.34.gu, bf16[128,128,128]{2,1,0:T(8,128)(2,1)S(1)} %copy-done, bf16[128,128,128]{2,1,0:T(8,128)(2,1)S(1)} %copy-done.1), custom_call_target="tpu_custom_call" | custom-call | flops 1610612736 | bytes 10485760 | tf_op jit(solution)/shard_map/terms/pallas_call | solution.py:92
  54.3 2.2 %collective-permute-done.14 = bf16[4,384,128]{2,1,0:T(8,128)(2,1)S(1)} collective-permute-done((bf16[4,384,128]{2,1,0:T(8,128)(2,1)S(1)}, bf16[4,384,128]{2,1,0:T(8,128)(2,1)S(1)}, u32[]{:S(2)}, u32[]{:S(2)}) %collective-permute-start.14) | collective-permute-done | bytes 393248 | tf_op jit(solution)/shard_map/ppermute | solution.py:35
  61.5 10.2 %collective-permute-done.5 = bf16[8,384,256]{2,1,0:T(8,128)(2,1)S(1)} collective-permute-done((bf16[8,384,256]{2,1,0:T(8,128)(2,1)S(1)}, bf16[8,384,256]{2,1,0:T(8,128)(2,1)S(1)}, u32[]{:S(2)}, u32[]{:S(2)}) %collective-permute-start.5) | collective-permute-done | bytes 1572896 | tf_op jit(solution)/shard_map/ppermute | solution.py:35
  73.2 5.4 %collective-permute-done.15.e1 = bf16[16,384,128]{2,1,0:T(8,128)(2,1)} collective-permute-done((bf16[16,384,128]{2,1,0:T(8,128)(2,1)S(1)}, bf16[16,384,128]{2,1,0:T(8,128)(2,1)}, u32[]{:S(2)}, u32[]{:S(2)}) %collective-permute-start.15) | collective-permute-done | bytes 1572896 | tf_op jit(solution)/shard_map/ppermute | solution.py:35
  82.9 5.3 %collective-permute-start.26 = (bf16[16,384,128]{2,1,0:T(8,128)(2,1)}, bf16[16,384,128]{2,1,0:T(8,128)(2,1)}, u32[]{:S(2)}, u32[]{:S(2)}) collective-permute-start(bf16[16,384,128]{2,1,0:T(8,128)(2,1)} %collective-permute-done.15.e1), channel_id=1, source_target_pairs={{0,32},{32,0},{1,33},{33,1},{2,34},{34,2},{3,35},{35,3},{4,36},{36... | collective-permute-start | bytes 4718600 | tf_op jit(solution)/shard_map/ppermute | solution.py:23
  88.3 12.3 %collective-permute-done.16.e2 = bf16[16,384,128]{2,1,0:T(8,128)(2,1)} collective-permute-done((bf16[16,384,128]{2,1,0:T(8,128)(2,1)}, bf16[16,384,128]{2,1,0:T(8,128)(2,1)}, u32[]{:S(2)}, u32[]{:S(2)}) %collective-permute-start.16) | collective-permute-done | bytes 1572896 | tf_op jit(solution)/shard_map/ppermute | solution.py:35
  100.6 3.1 %collective-permute-done.21.o2 = bf16[16,384,128]{2,1,0:T(8,128)(2,1)} collective-permute-done((bf16[16,384,128]{2,1,0:T(8,128)(2,1)}, bf16[16,384,128]{2,1,0:T(8,128)(2,1)}, u32[]{:S(2)}, u32[]{:S(2)}) %collective-permute-start.21) | collective-permute-done | bytes 1572896 | tf_op jit(solution)/shard_map/ppermute | solution.py:35
  103.8 2.3 %add_convert_fusion = bf16[8,384,256]{2,1,0:T(8,128)(2,1)S(1)} fusion(bf16[8,384,256]{2,1,0:T(8,128)(2,1)} %copy-done.2, bf16[8,384,256]{2,1,0:T(8,128)(2,1)} %collective-permute-done.8), kind=kLoop, calls=%fused_computation.1 | loop fusion | flops 3145728 | bytes 4718592 | tf_op jit(solution)/shard_map/convert_element_type | solution.py:39
  114.1 2.3 %collective-permute-done.11 = bf16[2,384,256]{2,1,0:T(8,128)(2,1)} collective-permute-done((bf16[2,384,256]{2,1,0:T(8,128)(2,1)S(1)}, bf16[2,384,256]{2,1,0:T(8,128)(2,1)}, u32[]{:S(2)}, u32[]{:S(2)}) %collective-permute-start.11) | collective-permute-done | bytes 393248 | tf_op jit(solution)/shard_map/ppermute | solution.py:35
  123.8 12.6 %early_grads.1 = (bf16[128,128,128]{2,1,0:T(8,128)(2,1)}, bf16[128,128,128]{2,1,0:T(8,128)(2,1)}) custom-call(s32[152]{0:T(256)S(1)} %get-tuple-element.57.lrow, s32[152]{0:T(256)S(1)} %get-tuple-element.56.lslot, s32[608]{0:T(1024)S(1)} %reshape.557.ltile, s32[10]{0:T(128)S(1)} %pad_add_fusion.1.meta, bf16[4,1024,384]{2,1,0:T(8,128)(2,1)S(1)} %pad_maximum_fusion.gt, ...), custom_call_target="tpu_custom_call" | custom-call | flops 6442450944 | bytes 23068672 | tf_op jit(solution)/shard_map/early_grads/pallas_call | solution.py:167
  136.4 2.1 %collective-permute-done.12 = bf16[2,384,256]{2,1,0:T(8,128)(2,1)S(1)} collective-permute-done((bf16[2,384,256]{2,1,0:T(8,128)(2,1)S(1)}, bf16[2,384,256]{2,1,0:T(8,128)(2,1)S(1)}, u32[]{:S(2)}, u32[]{:S(2)}) %collective-permute-start.12) | collective-permute-done | bytes 393248 | tf_op jit(solution)/shard_map/ppermute | solution.py:35
  139.1 8.6 %collective-permute-done.24 = bf16[2,384,256]{2,1,0:T(8,128)(2,1)S(1)} collective-permute-done((bf16[2,384,256]{2,1,0:T(8,128)(2,1)S(1)}, bf16[2,384,256]{2,1,0:T(8,128)(2,1)S(1)}, u32[]{:S(2)}, u32[]{:S(2)}) %collective-permute-start.24) | collective-permute-done | bytes 393248 | tf_op jit(solution)/shard_map/ppermute | solution.py:35
  148.3 2.6 %collective-permute-start.25 = (bf16[384,256]{1,0:T(8,128)(2,1)S(1)}, bf16[384,256]{1,0:T(8,128)(2,1)S(1)}, u32[]{:S(2)}, u32[]{:S(2)}) collective-permute-start(bf16[384,256]{1,0:T(8,128)(2,1)S(1)} %fusion), channel_id=1, source_target_pairs={{0,1},{1,0},{2,3},{3,2},{4,5},{5,4},{6,7},{7,6},{8,9},{9,8},{10,11... | collective-permute-start | bytes 589832 | tf_op jit(solution)/shard_map/ppermute | solution.py:23
  150.9 5.2 %collective-permute-done.25 = bf16[384,256]{1,0:T(8,128)(2,1)S(1)} collective-permute-done((bf16[384,256]{1,0:T(8,128)(2,1)S(1)}, bf16[384,256]{1,0:T(8,128)(2,1)S(1)}, u32[]{:S(2)}, u32[]{:S(2)}) %collective-permute-start.25) | collective-permute-done | bytes 196640 | tf_op jit(solution)/shard_map/ppermute | solution.py:23
  156.8 14.2 %late_grads.1 = (bf16[128,128,128]{2,1,0:T(8,128)(2,1)}, bf16[128,128,128]{2,1,0:T(8,128)(2,1)}) custom-call(s32[152]{0:T(256)S(1)} %get-tuple-element.57.lrow, s32[152]{0:T(256)S(1)} %get-tuple-element.56.lslot, s32[608]{0:T(1024)S(1)} %reshape.557.ltile, s32[10]{0:T(128)S(1)} %pad_add_fusion.1.meta, ...), custom_call_target="tpu_custom_call", output_to_operand_aliasing={{0}: (13, {}), {1}: (14, {})} | custom-call | flops 6442450944 | bytes 23068672 | tf_op jit(solution)/shard_map/late_grads/pallas_call | solution.py:167
  (135 shorter events, 49.5 us)
Async XLA Ops:
  1.6 24.1 %collective-permute-start.3 = (bf16[2,384,128]{2,1,0:T(8,128)(2,1)S(1)}, bf16[2,384,128]{2,1,0:T(8,128)(2,1)S(1)}, u32[]{:S(2)}, u32[]{:S(2)}) collective-permute-start(bf16[2,384,128]{2,1,0:T(8,128)(2,1)S(1)} %pad_maximum_fusion.6), channel_id=1, source_target_pairs={{0,24},{8,0},{16,8},{24,16},{32,40},{40,48},{48,56},{56,32},{1,25}... | collective-permute-start | bytes 589832 | tf_op jit(solution)/shard_map/ppermute | solution.py:35
  4.6 21.2 %collective-permute-start.2 = (bf16[2,384,128]{2,1,0:T(8,128)(2,1)S(1)}, bf16[2,384,128]{2,1,0:T(8,128)(2,1)S(1)}, u32[]{:S(2)}, u32[]{:S(2)}) collective-permute-start(bf16[2,384,128]{2,1,0:T(8,128)(2,1)S(1)} %pad_maximum_fusion.6), channel_id=1, source_target_pairs={{0,16},{8,24},{16,0},{24,8},{32,48},{40,56},{48,32},{56,40},{1,17}... | collective-permute-start | bytes 589832 | tf_op jit(solution)/shard_map/ppermute | solution.py:35
  5.4 20.4 %collective-permute-start.1 = (bf16[2,384,128]{2,1,0:T(8,128)(2,1)S(1)}, bf16[2,384,128]{2,1,0:T(8,128)(2,1)S(1)}, u32[]{:S(2)}, u32[]{:S(2)}) collective-permute-start(bf16[2,384,128]{2,1,0:T(8,128)(2,1)S(1)} %pad_maximum_fusion.6), channel_id=1, source_target_pairs={{0,8},{8,16},{16,24},{24,0},{32,56},{40,32},{48,40},{56,48},{1,9},... | collective-permute-start | bytes 589832 | tf_op jit(solution)/shard_map/ppermute | solution.py:35
  10.4 21.2 %collective-permute-start.4 = (bf16[1024,384]{1,0:T(8,128)(2,1)S(1)}, bf16[1024,384]{1,0:T(8,128)(2,1)S(1)}, u32[]{:S(2)}, u32[]{:S(2)}) collective-permute-start(bf16[1024,384]{1,0:T(8,128)(2,1)S(1)} %get-tuple-element.31), channel_id=1, source_target_pairs={{0,64},{64,0},{1,65},{65,1},{2,66},{66,2},{3,67},{67,3},{4,68},{68... | collective-permute-start | bytes 2359304 | tf_op jit(solution)/shard_map/ppermute | solution.py:23
  23.9 25.8 %collective-permute-start = (bf16[8,384,256]{2,1,0:T(8,128)(2,1)S(1)}, bf16[8,384,256]{2,1,0:T(8,128)(2,1)S(1)}, u32[]{:S(2)}, u32[]{:S(2)}) collective-permute-start(bf16[8,384,256]{2,1,0:T(8,128)(2,1)S(1)} %terms.4), channel_id=1, source_target_pairs={{0,8},{8,16},{16,24},{24,0},{32,56},{40,32},{48,40},{56,48},{1,9},... | collective-permute-start | bytes 4718600 | tf_op jit(solution)/shard_map/ppermute | solution.py:35
  25.9 11.7 %collective-permute-start.6 = (bf16[4,384,128]{2,1,0:T(8,128)(2,1)S(1)}, bf16[4,384,128]{2,1,0:T(8,128)(2,1)S(1)}, u32[]{:S(2)}, u32[]{:S(2)}) collective-permute-start(bf16[4,384,128]{2,1,0:T(8,128)(2,1)S(1)} %pad_maximum_fusion.4), channel_id=1, source_target_pairs={{0,2},{2,4},{4,6},{6,0},{32,38},{34,32},{36,34},{38,36},{1,3},{3,5... | collective-permute-start | bytes 1179656 | tf_op jit(solution)/shard_map/ppermute | solution.py:35
  33.4 25.8 %collective-permute-start.13 = (bf16[2,1024,384]{2,1,0:T(8,128)(2,1)S(1)}, bf16[2,1024,384]{2,1,0:T(8,128)(2,1)S(1)}, u32[]{:S(2)}, u32[]{:S(2)}) collective-permute-start(bf16[2,1024,384]{2,1,0:T(8,128)(2,1)S(1)} %pad_maximum_fusion.1), channel_id=1, source_target_pairs={{0,32},{32,0},{1,33},{33,1},{2,34},{34,2},{3,35},{35,3},{4,36},{36... | collective-permute-start | bytes 4718600 | tf_op jit(solution)/shard_map/ppermute | solution.py:23
  37.6 9.9 %collective-permute-start.9 = (bf16[4,384,128]{2,1,0:T(8,128)(2,1)S(1)}, bf16[4,384,128]{2,1,0:T(8,128)(2,1)S(1)}, u32[]{:S(2)}, u32[]{:S(2)}) collective-permute-start(bf16[4,384,128]{2,1,0:T(8,128)(2,1)S(1)} %collective-permute-done.6), channel_id=1, source_target_pairs={{0,2},{2,4},{4,6},{6,0},{32,38},{34,32},{36,34},{38,36},{1,3},{3,5... | collective-permute-start | bytes 1179656 | tf_op jit(solution)/shard_map/ppermute | solution.py:35
  50.0 21.7 %collective-permute-start.5 = (bf16[8,384,256]{2,1,0:T(8,128)(2,1)S(1)}, bf16[8,384,256]{2,1,0:T(8,128)(2,1)S(1)}, u32[]{:S(2)}, u32[]{:S(2)}) collective-permute-start(bf16[8,384,256]{2,1,0:T(8,128)(2,1)S(1)} %add_convert_fusion.2), channel_id=1, source_target_pairs={{0,8},{8,16},{16,24},{24,0},{32,56},{40,32},{48,40},{56,48},{1,9},... | collective-permute-start | bytes 4718600 | tf_op jit(solution)/shard_map/ppermute | solution.py:35
  56.7 21.9 %collective-permute-start.19 = (bf16[16,384,128]{2,1,0:T(8,128)(2,1)S(1)}, bf16[16,384,128]{2,1,0:T(8,128)(2,1)S(1)}, u32[]{:S(2)}, u32[]{:S(2)}) collective-permute-start(bf16[16,384,128]{2,1,0:T(8,128)(2,1)S(1)} %pad_maximum_fusion.2.e0), channel_id=1, source_target_pairs={{0,32},{32,0},{1,33},{33,1},{2,34},{34,2},{3,35},{35,3},{4,36},{36... | collective-permute-start | bytes 4718600 | tf_op jit(solution)/shard_map/ppermute | solution.py:23
  56.8 21.8 %collective-permute-start.15 = (bf16[16,384,128]{2,1,0:T(8,128)(2,1)S(1)}, bf16[16,384,128]{2,1,0:T(8,128)(2,1)}, u32[]{:S(2)}, u32[]{:S(2)}) collective-permute-start(bf16[16,384,128]{2,1,0:T(8,128)(2,1)S(1)} %pad_maximum_fusion.2.e0), channel_id=1, source_target_pairs={{0,1},{1,64},{32,97},{33,32},{64,65},{65,0},{96,33},{97,96},{2,3},... | collective-permute-start | bytes 4718600 | tf_op jit(solution)/shard_map/ppermute | solution.py:35
  58.8 21.0 %collective-permute-start.20 = (bf16[16,384,128]{2,1,0:T(8,128)(2,1)S(1)}, bf16[16,384,128]{2,1,0:T(8,128)(2,1)S(1)}, u32[]{:S(2)}, u32[]{:S(2)}) collective-permute-start(bf16[16,384,128]{2,1,0:T(8,128)(2,1)S(1)} %pad_maximum_fusion.3.o0), channel_id=1, source_target_pairs={{0,32},{32,0},{1,33},{33,1},{2,34},{34,2},{3,35},{35,3},{4,36},{36... | collective-permute-start | bytes 4718600 | tf_op jit(solution)/shard_map/ppermute | solution.py:23
  59.2 22.6 %collective-permute-start.18 = (bf16[16,384,128]{2,1,0:T(8,128)(2,1)S(1)}, bf16[16,384,128]{2,1,0:T(8,128)(2,1)}, u32[]{:S(2)}, u32[]{:S(2)}) collective-permute-start(bf16[16,384,128]{2,1,0:T(8,128)(2,1)S(1)} %pad_maximum_fusion.3.o0), channel_id=1, source_target_pairs={{0,2},{2,4},{4,6},{6,0},{32,38},{34,32},{36,34},{38,36},{1,3},{3,5... | collective-permute-start | bytes 4718600 | tf_op jit(solution)/shard_map/ppermute | solution.py:35
  78.6 21.9 %collective-permute-start.16 = (bf16[16,384,128]{2,1,0:T(8,128)(2,1)}, bf16[16,384,128]{2,1,0:T(8,128)(2,1)}, u32[]{:S(2)}, u32[]{:S(2)}) collective-permute-start(bf16[16,384,128]{2,1,0:T(8,128)(2,1)} %collective-permute-done.15.e1), channel_id=1, source_target_pairs={{0,1},{1,64},{32,97},{33,32},{64,65},{65,0},{96,33},{97,96},{2,3},... | collective-permute-start | bytes 4718600 | tf_op jit(solution)/shard_map/ppermute | solution.py:35
  81.7 21.9 %collective-permute-start.21 = (bf16[16,384,128]{2,1,0:T(8,128)(2,1)}, bf16[16,384,128]{2,1,0:T(8,128)(2,1)}, u32[]{:S(2)}, u32[]{:S(2)}) collective-permute-start(bf16[16,384,128]{2,1,0:T(8,128)(2,1)} %collective-permute-done.18.o1), channel_id=1, source_target_pairs={{0,2},{2,4},{4,6},{6,0},{32,38},{34,32},{36,34},{38,36},{1,3},{3,5... | collective-permute-start | bytes 4718600 | tf_op jit(solution)/shard_map/ppermute | solution.py:35
  81.7 22.0 %collective-permute-start.8 = (bf16[8,384,256]{2,1,0:T(8,128)(2,1)}, bf16[8,384,256]{2,1,0:T(8,128)(2,1)}, u32[]{:S(2)}, u32[]{:S(2)}) collective-permute-start(bf16[8,384,256]{2,1,0:T(8,128)(2,1)} %add_convert_fusion.1), channel_id=1, source_target_pairs={{0,8},{8,16},{16,24},{24,0},{32,56},{40,32},{48,40},{56,48},{1,9},... | collective-permute-start | bytes 4718600 | tf_op jit(solution)/shard_map/ppermute | solution.py:35
  82.9 28.9 %collective-permute-start.26 = (bf16[16,384,128]{2,1,0:T(8,128)(2,1)}, bf16[16,384,128]{2,1,0:T(8,128)(2,1)}, u32[]{:S(2)}, u32[]{:S(2)}) collective-permute-start(bf16[16,384,128]{2,1,0:T(8,128)(2,1)} %collective-permute-done.15.e1), channel_id=1, source_target_pairs={{0,32},{32,0},{1,33},{33,1},{2,34},{34,2},{3,35},{35,3},{4,36},{36... | collective-permute-start | bytes 4718600 | tf_op jit(solution)/shard_map/ppermute | solution.py:23
  88.2 24.2 %collective-permute-start.28 = (bf16[16,384,128]{2,1,0:T(8,128)(2,1)}, bf16[16,384,128]{2,1,0:T(8,128)(2,1)}, u32[]{:S(2)}, u32[]{:S(2)}) collective-permute-start(bf16[16,384,128]{2,1,0:T(8,128)(2,1)} %collective-permute-done.18.o1), channel_id=1, source_target_pairs={{0,32},{32,0},{1,33},{33,1},{2,34},{34,2},{3,35},{35,3},{4,36},{36... | collective-permute-start | bytes 4718600 | tf_op jit(solution)/shard_map/ppermute | solution.py:23
  100.6 17.6 %collective-permute-start.22 = (bf16[16,384,128]{2,1,0:T(8,128)(2,1)}, bf16[16,384,128]{2,1,0:T(8,128)(2,1)}, u32[]{:S(2)}, u32[]{:S(2)}) collective-permute-start(bf16[16,384,128]{2,1,0:T(8,128)(2,1)} %collective-permute-done.16.e2), channel_id=1, source_target_pairs={{0,32},{32,0},{1,33},{33,1},{2,34},{34,2},{3,35},{35,3},{4,36},{36... | collective-permute-start | bytes 4718600 | tf_op jit(solution)/shard_map/ppermute | solution.py:23
  103.7 14.5 %collective-permute-start.23 = (bf16[16,384,128]{2,1,0:T(8,128)(2,1)}, bf16[16,384,128]{2,1,0:T(8,128)(2,1)}, u32[]{:S(2)}, u32[]{:S(2)}) collective-permute-start(bf16[16,384,128]{2,1,0:T(8,128)(2,1)} %collective-permute-done.21.o2), channel_id=1, source_target_pairs={{0,32},{32,0},{1,33},{33,1},{2,34},{34,2},{3,35},{35,3},{4,36},{36... | collective-permute-start | bytes 4718600 | tf_op jit(solution)/shard_map/ppermute | solution.py:23
  107.2 9.2 %collective-permute-start.11 = (bf16[2,384,256]{2,1,0:T(8,128)(2,1)S(1)}, bf16[2,384,256]{2,1,0:T(8,128)(2,1)}, u32[]{:S(2)}, u32[]{:S(2)}) collective-permute-start(bf16[2,384,256]{2,1,0:T(8,128)(2,1)S(1)} %slice.69), channel_id=1, source_target_pairs={{0,2},{2,4},{4,6},{6,0},{32,38},{34,32},{36,34},{38,36},{1,3},{3,5... | collective-permute-start | bytes 1179656 | tf_op jit(solution)/shard_map/ppermute | solution.py:35
  111.7 36.0 %collective-permute-start.27 = (bf16[16,384,128]{2,1,0:T(8,128)(2,1)}, bf16[16,384,128]{2,1,0:T(8,128)(2,1)S(1)}, u32[]{:S(2)}, u32[]{:S(2)}) collective-permute-start(bf16[16,384,128]{2,1,0:T(8,128)(2,1)} %collective-permute-done.16.e2), channel_id=1, source_target_pairs={{0,1},{1,64},{32,97},{33,32},{64,65},{65,0},{96,33},{97,96},{2,3},... | collective-permute-start | bytes 4718600 | tf_op jit(solution)/shard_map/ppermute | solution.py:35
  112.5 35.4 %collective-permute-start.29 = (bf16[16,384,128]{2,1,0:T(8,128)(2,1)}, bf16[16,384,128]{2,1,0:T(8,128)(2,1)S(1)}, u32[]{:S(2)}, u32[]{:S(2)}) collective-permute-start(bf16[16,384,128]{2,1,0:T(8,128)(2,1)} %collective-permute-done.21.o2), channel_id=1, source_target_pairs={{0,2},{2,4},{4,6},{6,0},{32,38},{34,32},{36,34},{38,36},{1,3},{3,5... | collective-permute-start | bytes 4718600 | tf_op jit(solution)/shard_map/ppermute | solution.py:35
  117.6 20.9 %collective-permute-start.12 = (bf16[2,384,256]{2,1,0:T(8,128)(2,1)S(1)}, bf16[2,384,256]{2,1,0:T(8,128)(2,1)S(1)}, u32[]{:S(2)}, u32[]{:S(2)}) collective-permute-start(bf16[2,384,256]{2,1,0:T(8,128)(2,1)S(1)} %add_convert_fusion.4), channel_id=1, source_target_pairs={{0,2},{2,4},{4,6},{6,0},{32,38},{34,32},{36,34},{38,36},{1,3},{3,5... | collective-permute-start | bytes 1179656 | tf_op jit(solution)/shard_map/ppermute | solution.py:35
  (30 other events, 170.1 us)
